TPU v7x, 32 devices: a whole 2x2x4 slice. The times are simulated.
32 devices in a mesh: row: 2 (over core), ax: 2 (over x), az: 8 (over z, y).
Axes of the slice: x: 2, y: 2, z: 4, core: 2. Of those that a mesh axis runs over, the one named last changes fastest.
Arguments:
- density: float32 [2, 4, 256, 512], P('row', 'ax', 'az'), may hold values from 0.8 to 1.6
- velocity: float32 [2, 3, 4, 256, 512], P('row', None, 'ax', 'az'), may hold values from -1.5 to 1.5
- pressure: float32 [2, 4, 256, 512], P('row', 'ax', 'az'), may hold values from 0.4 to 1.2
- offsets: int32 [3], replicated, may hold values from 0 to 255
Outputs:
- final_state: float32 [2, 5, 4, 256, 512], P('row', None, 'ax', 'az')
All inputs are finite; a program needn't handle non-finite values.
Results may differ from a plain program's by a relative error of at most 0.00002.
Values sent between devices are 32-bit elements; how exact they have to be, the bound alone decides.
A program may use at most 128 MiB of HBM per device.

v0:
```python
import math

import jax
import jax.numpy as jnp
from jax import lax
from jax.sharding import PartitionSpec as P

HEAT_RATIO = 1.4
VISCOSITY = 0.8
CONDUCTION = 0.6
TIME_STEP = 0.1
AXIAL_FLUX = 1.0
AXIAL_CURVE = 4.0


def partner_2(value, axis, bit):
    mask = 2**bit
    pairs = [(source, source ^ mask) for source in range(lax.axis_size(axis))]
    return lax.ppermute(value, axis, pairs)


def padded(cells, sides, width, closed):
    for axis, dim in sides:
        count = lax.axis_size(axis)
        ends = count if closed else count - 1
        head = lax.slice_in_dim(cells, 0, width, axis=dim)
        tail = lax.slice_in_dim(cells, cells.shape[dim] - width, cells.shape[dim], axis=dim)
        cells = jnp.concatenate(
            [
                lax.ppermute(tail, axis, [(i, (i + 1) % count) for i in range(ends)]),
                cells,
                lax.ppermute(head, axis, [((i + 1) % count, i) for i in range(ends)]),
            ],
            axis=dim,
        )
    return cells


def conserved(density, velocity, pressure):
    momentum = density[:, None] * velocity
    energy = pressure / (HEAT_RATIO - 1.0) + 0.5 * density * jnp.sum(velocity * velocity, axis=1)
    return jnp.concatenate([density[:, None], momentum, energy[:, None]], axis=1)


def primitive(state):
    vel_theta = state[:, 1] / state[:, 0]
    vel_radial = state[:, 2] / state[:, 0]
    vel_axial = state[:, 3] / state[:, 0]
    press = (HEAT_RATIO - 1.0) * (
        state[:, 4]
        - 0.5 * (state[:, 1] * vel_theta + state[:, 2] * vel_radial + state[:, 3] * vel_axial)
    )
    return (vel_theta, vel_radial, vel_axial, press / state[:, 0], press)


def fluxes(state, values, direction):
    normal_vel = values[direction]
    press = values[4]
    flux_terms = [
        state[:, 0] * normal_vel,
        state[:, 1] * normal_vel,
        state[:, 2] * normal_vel,
        state[:, 3] * normal_vel,
        (state[:, 4] + press) * normal_vel,
    ]
    flux_terms[1 + direction] = flux_terms[1 + direction] + press
    return flux_terms


def extended(state, values_c, lower, upper, axis_pos):
    values_lo = primitive(lower)
    values_hi = primitive(upper)
    ext_state = jnp.concatenate([lower, state, upper], axis=axis_pos)
    ext_values = tuple(
        (
            jnp.concatenate([values_lo[k], values_c[k], values_hi[k]], axis=axis_pos - 1)
            for k in range(5)
        )
    )
    return (ext_state, ext_values)


def side_slices(items, axis_pos):
    size_now = items[0].shape[axis_pos] - 2
    lows = [lax.slice_in_dim(item, 0, size_now, axis=axis_pos) for item in items]
    highs = [lax.slice_in_dim(item, 2, size_now + 2, axis=axis_pos) for item in items]
    return (lows, highs)


def tendency(state, theta_ghosts, radial_ghosts, axial_ghosts, radius, dtheta):
    values_c = primitive(state)
    directions = [(theta_ghosts, 3), (radial_ghosts, 4), (axial_ghosts, 2)]
    flux_lo = []
    flux_hi = []
    value_lo = []
    value_hi = []
    for direction_index in range(3):
        ghosts, axis_pos = directions[direction_index]
        ext_state, ext_values = extended(state, values_c, ghosts[0], ghosts[1], axis_pos)
        flux_all = fluxes(ext_state, ext_values, direction_index)
        lows, highs = side_slices(flux_all, axis_pos - 1)
        flux_lo.append(lows)
        flux_hi.append(highs)
        vlows, vhighs = side_slices(list(ext_values), axis_pos - 1)
        value_lo.append(vlows)
        value_hi.append(vhighs)
    result = []
    for field_index in range(5):
        divergence = -(flux_hi[0][field_index] - flux_lo[0][field_index]) / (2.0 * radius * dtheta)
        divergence = divergence - (
            (radius + 1.0) * flux_hi[1][field_index] - (radius - 1.0) * flux_lo[1][field_index]
        ) / (2.0 * radius)
        divergence = divergence - AXIAL_FLUX * (flux_hi[2][field_index] - flux_lo[2][field_index])
        result.append(divergence)

    def viscous(which):
        center = values_c[which]
        beside_all = (value_hi[0][which] - 2.0 * center + value_lo[0][which]) / (
            radius * dtheta
        ) ** 2
        across = (
            (radius + 0.5) * (value_hi[1][which] - center)
            - (radius - 0.5) * (center - value_lo[1][which])
        ) / radius
        return (
            beside_all
            + across
            + AXIAL_CURVE * (value_hi[2][which] - 2.0 * center + value_lo[2][which])
        )

    density_now = state[:, 0]
    result[1] = (
        result[1]
        - density_now * values_c[0] * values_c[1] / radius
        + VISCOSITY
        * (
            viscous(0)
            - values_c[0] / radius**2
            + (value_hi[0][1] - value_lo[0][1]) / (radius**2 * dtheta)
        )
    )
    result[2] = (
        result[2]
        + (density_now * values_c[0] * values_c[0] + values_c[4]) / radius
        + VISCOSITY
        * (
            viscous(1)
            - values_c[1] / radius**2
            - (value_hi[0][0] - value_lo[0][0]) / (radius**2 * dtheta)
        )
    )
    result[3] = result[3] + VISCOSITY * viscous(2)
    result[4] = result[4] + CONDUCTION * viscous(3)
    return jnp.stack(result, axis=1)


def body(density, velocity, pressure, offsets):
    state0 = conserved(density, velocity, pressure)
    tile_cells = state0.shape[3]
    radial_cells = state0.shape[4]
    cycle_size = lax.axis_size("az")
    cycle_cells = tile_cells * cycle_size
    dtheta = 2.0 * math.pi / cycle_cells
    radius = cycle_cells / (2.0 * math.pi) + jnp.arange(radial_cells, dtype=jnp.float32) + 0.5
    at_outer = lax.axis_index("ax") == 0
    at_plane = lax.axis_index("ax") == lax.axis_size("ax") - 1
    is_rotor = lax.axis_index("row") == 0
    axial_sign = jnp.array([1.0, 1.0, 1.0, -1.0, 1.0], dtype=jnp.float32).reshape(5, 1, 1)
    wall_sign = jnp.array([1.0, -1.0, -1.0, -1.0, 1.0], dtype=jnp.float32).reshape(5, 1, 1, 1)

    def rotate_plane(partner, turn_cells):
        band = lax.all_to_all(partner, "az", split_axis=2, concat_axis=1, tiled=True)
        doubled = jnp.concatenate([band, band], axis=1)
        rolled = lax.dynamic_slice_in_dim(doubled, turn_cells, cycle_cells, 1)
        return lax.all_to_all(rolled, "az", split_axis=1, concat_axis=2, tiled=True)

    def full_rate(state, shift):
        top_plane = state[0, :, -1] * axial_sign
        partner = partner_2(top_plane, "row", 0)
        turn_cells = jnp.where(is_rotor, shift, (cycle_cells - shift) % cycle_cells)
        ghost_plane = rotate_plane(partner, turn_cells)
        cycle_pad = padded(state, (("az", 3),), 1, True)
        theta_lo = cycle_pad[:, :, :, :1]
        theta_hi = cycle_pad[:, :, :, -1:]
        plane_pad = padded(state, (("ax", 2),), 1, False)
        lower_ghost = plane_pad[:, :, :1]
        upper_ghost = plane_pad[:, :, -1:]
        lower_ghost = jnp.where(at_outer, state[:, :, :1], lower_ghost)
        upper_ghost = jnp.where(at_plane, ghost_plane[None, :, None], upper_ghost)
        radial_lo = state[..., :1] * wall_sign
        radial_hi = state[..., -1:] * wall_sign
        return tendency(
            state,
            (theta_lo, theta_hi),
            (radial_lo, radial_hi),
            (lower_ghost, upper_ghost),
            radius,
            dtheta,
        )

    state1 = state0 + TIME_STEP * full_rate(state0, offsets[0])
    state2 = 0.75 * state0 + 0.25 * (state1 + TIME_STEP * full_rate(state1, offsets[1]))
    return state0 / 3.0 + 2.0 / 3.0 * (state2 + TIME_STEP * full_rate(state2, offsets[2]))


def solution(mesh):
    placed = (
        P("row", "ax", "az", None),
        P("row", None, "ax", "az", None),
        P("row", "ax", "az", None),
        P(),
    )
    return jax.shard_map(
        body,
        mesh=mesh,
        in_specs=placed,
        out_specs=P("row", None, "ax", "az", None),
        check_vma=False,
    )
```

profile of v0, /device:TPU:0, one launch (start us, length us, event | category | flops | bytes accessed | tf_op | source)
XLA Modules:
  0.0 213.5 jit_solution(6756760806415778338)
XLA Ops:
  1.1 1.7 fusion.604
  4.3 5.1 %collective-permute-start.2 = (f32[1,5,1,32,512]{4,3,2,1,0:T(8,128)}, f32[1,5,1,32,512]{4,3,2,1,0:T(8,128)}, u32[]{:S(2)}, u32[]{:S(2)}) collective-permute-start(f32[1,5,1,32,512]{4,3,2,1,0:T(8,128)} %copy.605), channel_id=1, source_target_pairs={{0,8},{1,9},{2,10},{3,11},{4,12},{5,13},{6,14},{7,15},{16,24},{17,... | collective-permute-start | bytes 983048 | tf_op jit(solution)/shard_map/ppermute | solution.py:30
  11.1 3.2 %collective-permute-start.1 = (f32[1,5,2,1,512]{4,3,2,1,0:T(1,128)S(1)}, f32[1,5,2,1,512]{4,3,2,1,0:T(1,128)S(1)}, u32[]{:S(2)}, u32[]{:S(2)}) collective-permute-start(f32[1,5,2,1,512]{4,3,2,1,0:T(1,128)S(1)} %get-tuple-element.176), channel_id=1, source_target_pairs={{1,0},{2,1},{3,2},{4,3},{5,4},{6,5},{7,6},{0,7},{9,8},{10,9},{11,1... | collective-permute-start | bytes 61448 | tf_op jit(solution)/shard_map/ppermute | solution.py:32
  28.6 1.7 copy.397
  31.7 3.6 %all-to-all-start = ((f32[8,1,10240]{2,1,0:T(1,128)}), f32[8,1,10240]{2,1,0:T(1,128)S(1)}, u32[]{:S(2)}, u32[]{:S(2)}) async-start(f32[8,1,10240]{2,1,0:T(1,128)} %reshape.11896), calls=%async_computation | async-start | bytes 655360 | tf_op jit(solution)/shard_map/all_to_all | solution.py:172
  35.9 1.9 fusion.59
  38.5 7.3 %all-to-all-done = f32[8,1,10240]{2,1,0:T(1,128)S(1)} async-done(((f32[8,1,10240]{2,1,0:T(1,128)}), f32[8,1,10240]{2,1,0:T(1,128)S(1)}, u32[]{:S(2)}, u32[]{:S(2)}) %all-to-all-start) | async-done | bytes 327712 | tf_op jit(solution)/shard_map/all_to_all | solution.py:172
  46.4 2.2 %reduce.91 = f32[8,10240]{1,0:T(8,128)} reduce(f32[8,1,10240]{2,1,0:T(1,128)S(1)} %all-to-all-done, f32[]{:T(128)} %broadcast.1686), dimensions={1}, to_apply=%all_to_all.72.reduce_sub_computation | reduce | bytes 655364 | tf_op jit(solution)/shard_map/all_to_all | solution.py:172
  54.5 3.6 %all-to-all-start.1 = ((f32[8,1,10240]{2,1,0:T(1,128)}), f32[8,1,10240]{2,1,0:T(1,128)S(1)}, u32[]{:S(2)}, u32[]{:S(2)}) async-start(f32[8,1,10240]{2,1,0:T(1,128)} %reshape.11898), calls=%async_computation.1 | async-start | bytes 655360 | tf_op jit(solution)/shard_map/all_to_all | solution.py:175
  61.8 6.6 %all-to-all-done.1 = f32[8,1,10240]{2,1,0:T(1,128)S(1)} async-done(((f32[8,1,10240]{2,1,0:T(1,128)}), f32[8,1,10240]{2,1,0:T(1,128)S(1)}, u32[]{:S(2)}, u32[]{:S(2)}) %all-to-all-start.1) | async-done | bytes 327712 | tf_op jit(solution)/shard_map/all_to_all | solution.py:175
  80.2 2.0 collective-permute-start.7
  83.6 3.3 %collective-permute-start.6 = (f32[1,5,2,1,512]{4,3,2,1,0:T(1,128)S(1)}, f32[1,5,2,1,512]{4,3,2,1,0:T(1,128)S(1)}, u32[]{:S(2)}, u32[]{:S(2)}) collective-permute-start(f32[1,5,2,1,512]{4,3,2,1,0:T(1,128)S(1)} %get-tuple-element.172), channel_id=1, source_target_pairs={{1,0},{2,1},{3,2},{4,3},{5,4},{6,5},{7,6},{0,7},{9,8},{10,9},{11,1... | collective-permute-start | bytes 61448 | tf_op jit(solution)/shard_map/ppermute | solution.py:32
  96.6 1.8 copy.437
  99.8 3.6 %all-to-all-start.2 = ((f32[8,1,10240]{2,1,0:T(1,128)}), f32[8,1,10240]{2,1,0:T(1,128)S(1)}, u32[]{:S(2)}, u32[]{:S(2)}) async-start(f32[8,1,10240]{2,1,0:T(1,128)} %reshape.11900), calls=%async_computation.2 | async-start | bytes 655360 | tf_op jit(solution)/shard_map/all_to_all | solution.py:172
  104.7 2.0 fusion.45
  107.3 6.6 %all-to-all-done.2 = f32[8,1,10240]{2,1,0:T(1,128)S(1)} async-done(((f32[8,1,10240]{2,1,0:T(1,128)}), f32[8,1,10240]{2,1,0:T(1,128)S(1)}, u32[]{:S(2)}, u32[]{:S(2)}) %all-to-all-start.2) | async-done | bytes 327712 | tf_op jit(solution)/shard_map/all_to_all | solution.py:172
  113.9 2.2 %reduce.93 = f32[8,10240]{1,0:T(8,128)} reduce(f32[8,1,10240]{2,1,0:T(1,128)S(1)} %all-to-all-done.2, f32[]{:T(128)} %broadcast.1686), dimensions={1}, to_apply=%all_to_all.79.reduce_sub_computation | reduce | bytes 655364 | tf_op jit(solution)/shard_map/all_to_all | solution.py:172
  116.1 1.6 reshape.11901
  122.0 3.6 %all-to-all-start.3 = ((f32[8,1,10240]{2,1,0:T(1,128)}), f32[8,1,10240]{2,1,0:T(1,128)S(1)}, u32[]{:S(2)}, u32[]{:S(2)}) async-start(f32[8,1,10240]{2,1,0:T(1,128)} %reshape.11902), calls=%async_computation.3 | async-start | bytes 655360 | tf_op jit(solution)/shard_map/all_to_all | solution.py:175
  125.6 1.8 bitcast_select_fusion.2
  130.2 5.7 %all-to-all-done.3 = f32[8,1,10240]{2,1,0:T(1,128)S(1)} async-done(((f32[8,1,10240]{2,1,0:T(1,128)}), f32[8,1,10240]{2,1,0:T(1,128)S(1)}, u32[]{:S(2)}, u32[]{:S(2)}) %all-to-all-start.3) | async-done | bytes 327712 | tf_op jit(solution)/shard_map/all_to_all | solution.py:175
  148.9 2.0 collective-permute-start.12
  150.9 1.7 collective-permute-start.10
  152.6 3.0 %collective-permute-start.11 = (f32[1,5,2,1,512]{4,3,2,1,0:T(1,128)S(1)}, f32[1,5,2,1,512]{4,3,2,1,0:T(1,128)S(1)}, u32[]{:S(2)}, u32[]{:S(2)}) collective-permute-start(f32[1,5,2,1,512]{4,3,2,1,0:T(1,128)S(1)} %get-tuple-element.164), channel_id=1, source_target_pairs={{1,0},{2,1},{3,2},{4,3},{5,4},{6,5},{7,6},{0,7},{9,8},{10,9},{11,1... | collective-permute-start | bytes 61448 | tf_op jit(solution)/shard_map/ppermute | solution.py:32
  165.3 1.8 copy.470
  168.4 3.6 %all-to-all-start.4 = ((f32[8,1,10240]{2,1,0:T(1,128)}), f32[8,1,10240]{2,1,0:T(1,128)S(1)}, u32[]{:S(2)}, u32[]{:S(2)}) async-start(f32[8,1,10240]{2,1,0:T(1,128)} %reshape.11904), calls=%async_computation.4 | async-start | bytes 655360 | tf_op jit(solution)/shard_map/all_to_all | solution.py:172
  173.3 2.0 fusion.31
  175.9 6.6 %all-to-all-done.4 = f32[8,1,10240]{2,1,0:T(1,128)S(1)} async-done(((f32[8,1,10240]{2,1,0:T(1,128)}), f32[8,1,10240]{2,1,0:T(1,128)S(1)}, u32[]{:S(2)}, u32[]{:S(2)}) %all-to-all-start.4) | async-done | bytes 327712 | tf_op jit(solution)/shard_map/all_to_all | solution.py:172
  182.6 2.2 %reduce.95 = f32[8,10240]{1,0:T(8,128)} reduce(f32[8,1,10240]{2,1,0:T(1,128)S(1)} %all-to-all-done.4, f32[]{:T(128)} %broadcast.1686), dimensions={1}, to_apply=%all_to_all.86.reduce_sub_computation | reduce | bytes 655364 | tf_op jit(solution)/shard_map/all_to_all | solution.py:172
  184.8 1.6 reshape.11905
  190.6 3.6 %all-to-all-start.5 = ((f32[8,1,10240]{2,1,0:T(1,128)}), f32[8,1,10240]{2,1,0:T(1,128)S(1)}, u32[]{:S(2)}, u32[]{:S(2)}) async-start(f32[8,1,10240]{2,1,0:T(1,128)} %reshape.11906), calls=%async_computation.5 | async-start | bytes 655360 | tf_op jit(solution)/shard_map/all_to_all | solution.py:175
  198.0 6.7 %all-to-all-done.5 = f32[8,1,10240]{2,1,0:T(1,128)S(1)} async-done(((f32[8,1,10240]{2,1,0:T(1,128)}), f32[8,1,10240]{2,1,0:T(1,128)S(1)}, u32[]{:S(2)}, u32[]{:S(2)}) %all-to-all-start.5) | async-done | bytes 327712 | tf_op jit(solution)/shard_map/all_to_all | solution.py:175
  (497 shorter events, 101.5 us)
Async XLA Ops:
  3.0 25.6 %collective-permute-start.3 = (f32[5,32,512]{2,1,0:T(8,128)S(1)}, f32[5,32,512]{2,1,0:T(8,128)}, u32[]{:S(2)}, u32[]{:S(2)}) collective-permute-start(f32[5,32,512]{2,1,0:T(8,128)S(1)} %bitcast_multiply_fusion.2), channel_id=1, source_target_pairs={{0,16},{16,0},{1,17},{17,1},{2,18},{18,2},{3,19},{19,3},{4,20},{20... | collective-permute-start | bytes 983048 | tf_op jit(solution)/shard_map/ppermute | solution.py:19
  3.6 10.7 %copy-start.143 = (f32[5]{0:T(128)S(1)}, f32[5]{0:T(128)}, u32[]{:S(2)}) copy-start(f32[5]{0:T(128)} %constant.94.clone) | copy-start | bytes 64
  4.3 53.8 %collective-permute-start.2 = (f32[1,5,1,32,512]{4,3,2,1,0:T(8,128)}, f32[1,5,1,32,512]{4,3,2,1,0:T(8,128)}, u32[]{:S(2)}, u32[]{:S(2)}) collective-permute-start(f32[1,5,1,32,512]{4,3,2,1,0:T(8,128)} %copy.605), channel_id=1, source_target_pairs={{0,8},{1,9},{2,10},{3,11},{4,12},{5,13},{6,14},{7,15},{16,24},{17,... | collective-permute-start | bytes 983048 | tf_op jit(solution)/shard_map/ppermute | solution.py:30
  9.5 17.9 %collective-permute-start = (f32[1,5,2,1,512]{4,3,2,1,0:T(1,128)S(1)}, f32[1,5,2,1,512]{4,3,2,1,0:T(1,128)S(1)}, u32[]{:S(2)}, u32[]{:S(2)}) collective-permute-start(f32[1,5,2,1,512]{4,3,2,1,0:T(1,128)S(1)} %get-tuple-element.175), channel_id=1, source_target_pairs={{0,1},{1,2},{2,3},{3,4},{4,5},{5,6},{6,7},{7,0},{8,9},{9,10},{10,1... | collective-permute-start | bytes 61448 | tf_op jit(solution)/shard_map/ppermute | solution.py:30
  11.1 16.3 %collective-permute-start.1 = (f32[1,5,2,1,512]{4,3,2,1,0:T(1,128)S(1)}, f32[1,5,2,1,512]{4,3,2,1,0:T(1,128)S(1)}, u32[]{:S(2)}, u32[]{:S(2)}) collective-permute-start(f32[1,5,2,1,512]{4,3,2,1,0:T(1,128)S(1)} %get-tuple-element.176), channel_id=1, source_target_pairs={{1,0},{2,1},{3,2},{4,3},{5,4},{6,5},{7,6},{0,7},{9,8},{10,9},{11,1... | collective-permute-start | bytes 61448 | tf_op jit(solution)/shard_map/ppermute | solution.py:32
  15.0 60.4 %copy-start.50 = (f32[512]{0:T(512)}, f32[512]{0:T(512)S(1)}, u32[]{:S(2)}) copy-start(f32[512]{0:T(512)S(1)} %get-tuple-element.244) | copy-start | bytes 6148
  15.1 60.4 %copy-start.53 = (f32[512]{0:T(512)}, f32[512]{0:T(512)S(1)}, u32[]{:S(2)}) copy-start(f32[512]{0:T(512)S(1)} %get-tuple-element.245) | copy-start | bytes 6148
  15.1 60.4 %copy-start.56 = (f32[512]{0:T(512)}, f32[512]{0:T(512)S(1)}, u32[]{:S(2)}) copy-start(f32[512]{0:T(512)S(1)} %get-tuple-element.246) | copy-start | bytes 6148
  15.1 60.4 %copy-start.59 = (f32[512]{0:T(512)}, f32[512]{0:T(512)S(1)}, u32[]{:S(2)}) copy-start(f32[512]{0:T(512)S(1)} %get-tuple-element.247) | copy-start | bytes 6148
  17.9 56.4 %copy-start.108 = (f32[512]{0:T(512)}, f32[512]{0:T(512)S(1)}, u32[]{:S(2)}) copy-start(f32[512]{0:T(512)S(1)} %get-tuple-element.248) | copy-start | bytes 6148
  17.9 56.4 %copy-start.111 = (f32[512]{0:T(512)}, f32[512]{0:T(512)S(1)}, u32[]{:S(2)}) copy-start(f32[512]{0:T(512)S(1)} %get-tuple-element.249) | copy-start | bytes 6148
  31.7 14.0 %all-to-all-start = ((f32[8,1,10240]{2,1,0:T(1,128)}), f32[8,1,10240]{2,1,0:T(1,128)S(1)}, u32[]{:S(2)}, u32[]{:S(2)}) async-start(f32[8,1,10240]{2,1,0:T(1,128)} %reshape.11896), calls=%async_computation | async-start | bytes 655360 | tf_op jit(solution)/shard_map/all_to_all | solution.py:172
  54.5 13.9 %all-to-all-start.1 = ((f32[8,1,10240]{2,1,0:T(1,128)}), f32[8,1,10240]{2,1,0:T(1,128)S(1)}, u32[]{:S(2)}, u32[]{:S(2)}) async-start(f32[8,1,10240]{2,1,0:T(1,128)} %reshape.11898), calls=%async_computation.1 | async-start | bytes 655360 | tf_op jit(solution)/shard_map/all_to_all | solution.py:175
  58.9 11.8 %collective-permute-start.4 = (f32[1,5,1,32,512]{4,3,2,1,0:T(8,128)}, f32[1,5,1,32,512]{4,3,2,1,0:T(8,128)}, u32[]{:S(2)}, u32[]{:S(2)}) collective-permute-start(f32[1,5,1,32,512]{4,3,2,1,0:T(8,128)} %get-tuple-element.178), channel_id=1, source_target_pairs={{8,0},{9,1},{10,2},{11,3},{12,4},{13,5},{14,6},{15,7},{24,16},{25,... | collective-permute-start | bytes 983048 | tf_op jit(solution)/shard_map/ppermute | solution.py:32
  77.9 17.9 %copy-start.13 = (f32[1,2,32,512]{3,2,1,0:T(8,128)}, f32[1,2,32,512]{3,2,1,0:T(8,128)S(1)}, u32[]{:S(2)}) copy-start(f32[1,2,32,512]{3,2,1,0:T(8,128)S(1)} %get-tuple-element.170) | copy-start | bytes 393220
  80.1 16.5 %collective-permute-start.8 = (f32[5,32,512]{2,1,0:T(8,128)S(1)}, f32[5,32,512]{2,1,0:T(8,128)}, u32[]{:S(2)}, u32[]{:S(2)}) collective-permute-start(f32[5,32,512]{2,1,0:T(8,128)S(1)} %bitcast_multiply_fusion.1), channel_id=1, source_target_pairs={{0,16},{16,0},{1,17},{17,1},{2,18},{18,2},{3,19},{19,3},{4,20},{20... | collective-permute-start | bytes 983048 | tf_op jit(solution)/shard_map/ppermute | solution.py:19
  80.2 45.4 %collective-permute-start.7 = (f32[1,5,1,32,512]{4,3,1,2,0:T(8,128)}, f32[1,5,1,32,512]{4,3,1,2,0:T(8,128)}, u32[]{:S(2)}, u32[]{:S(2)}) collective-permute-start(f32[1,5,1,32,512]{4,3,1,2,0:T(8,128)} %slice.1633), channel_id=1, source_target_pairs={{0,8},{1,9},{2,10},{3,11},{4,12},{5,13},{6,14},{7,15},{16,24},{17,... | collective-permute-start | bytes 983048 | tf_op jit(solution)/shard_map/ppermute | solution.py:30
  82.2 12.8 %collective-permute-start.5 = (f32[1,5,2,1,512]{4,3,2,1,0:T(1,128)S(1)}, f32[1,5,2,1,512]{4,3,2,1,0:T(1,128)S(1)}, u32[]{:S(2)}, u32[]{:S(2)}) collective-permute-start(f32[1,5,2,1,512]{4,3,2,1,0:T(1,128)S(1)} %get-tuple-element.171), channel_id=1, source_target_pairs={{0,1},{1,2},{2,3},{3,4},{4,5},{5,6},{6,7},{7,0},{8,9},{9,10},{10,1... | collective-permute-start | bytes 61448 | tf_op jit(solution)/shard_map/ppermute | solution.py:30
  83.6 10.7 %collective-permute-start.6 = (f32[1,5,2,1,512]{4,3,2,1,0:T(1,128)S(1)}, f32[1,5,2,1,512]{4,3,2,1,0:T(1,128)S(1)}, u32[]{:S(2)}, u32[]{:S(2)}) collective-permute-start(f32[1,5,2,1,512]{4,3,2,1,0:T(1,128)S(1)} %get-tuple-element.172), channel_id=1, source_target_pairs={{1,0},{2,1},{3,2},{4,3},{5,4},{6,5},{7,6},{0,7},{9,8},{10,9},{11,1... | collective-permute-start | bytes 61448 | tf_op jit(solution)/shard_map/ppermute | solution.py:32
  99.8 6.9 %copy-start.79 = (f32[1,5,2,1,512]{4,3,2,1,0:T(1,128)S(1)}, f32[1,5,2,1,512]{4,3,2,1,0:T(1,128)}, u32[]{:S(2)}) copy-start(f32[1,5,2,1,512]{4,3,2,1,0:T(1,128)} %copy-done.78) | copy-start | bytes 61444
  99.8 14.1 %all-to-all-start.2 = ((f32[8,1,10240]{2,1,0:T(1,128)}), f32[8,1,10240]{2,1,0:T(1,128)S(1)}, u32[]{:S(2)}, u32[]{:S(2)}) async-start(f32[8,1,10240]{2,1,0:T(1,128)} %reshape.11900), calls=%async_computation.2 | async-start | bytes 655360 | tf_op jit(solution)/shard_map/all_to_all | solution.py:172
  122.0 14.0 %all-to-all-start.3 = ((f32[8,1,10240]{2,1,0:T(1,128)}), f32[8,1,10240]{2,1,0:T(1,128)S(1)}, u32[]{:S(2)}, u32[]{:S(2)}) async-start(f32[8,1,10240]{2,1,0:T(1,128)} %reshape.11902), calls=%async_computation.3 | async-start | bytes 655360 | tf_op jit(solution)/shard_map/all_to_all | solution.py:175
  127.4 11.5 %collective-permute-start.9 = (f32[1,5,1,32,512]{4,3,2,1,0:T(8,128)}, f32[1,5,1,32,512]{4,3,2,1,0:T(8,128)}, u32[]{:S(2)}, u32[]{:S(2)}) collective-permute-start(f32[1,5,1,32,512]{4,3,2,1,0:T(8,128)} %get-tuple-element.174), channel_id=1, source_target_pairs={{8,0},{9,1},{10,2},{11,3},{12,4},{13,5},{14,6},{15,7},{24,16},{25,... | collective-permute-start | bytes 983048 | tf_op jit(solution)/shard_map/ppermute | solution.py:32
  146.5 17.9 %copy-start.12 = (f32[1,2,32,512]{3,2,1,0:T(8,128)}, f32[1,2,32,512]{3,2,1,0:T(8,128)S(1)}, u32[]{:S(2)}) copy-start(f32[1,2,32,512]{3,2,1,0:T(8,128)S(1)} %get-tuple-element.162) | copy-start | bytes 393220
  148.0 17.2 %collective-permute-start.13 = (f32[5,32,512]{2,1,0:T(8,128)S(1)}, f32[5,32,512]{2,1,0:T(8,128)}, u32[]{:S(2)}, u32[]{:S(2)}) collective-permute-start(f32[5,32,512]{2,1,0:T(8,128)S(1)} %bitcast_multiply_fusion), channel_id=1, source_target_pairs={{0,16},{16,0},{1,17},{17,1},{2,18},{18,2},{3,19},{19,3},{4,20},{20... | collective-permute-start | bytes 983048 | tf_op jit(solution)/shard_map/ppermute | solution.py:19
  148.9 45.4 %collective-permute-start.12 = (f32[1,5,1,32,512]{4,3,2,1,0:T(8,128)}, f32[1,5,1,32,512]{4,3,2,1,0:T(8,128)}, u32[]{:S(2)}, u32[]{:S(2)}) collective-permute-start(f32[1,5,1,32,512]{4,3,2,1,0:T(8,128)} %copy.606), channel_id=1, source_target_pairs={{0,8},{1,9},{2,10},{3,11},{4,12},{5,13},{6,14},{7,15},{16,24},{17,... | collective-permute-start | bytes 983048 | tf_op jit(solution)/shard_map/ppermute | solution.py:30
  150.9 12.1 %collective-permute-start.10 = (f32[1,5,2,1,512]{4,3,2,1,0:T(1,128)S(1)}, f32[1,5,2,1,512]{4,3,2,1,0:T(1,128)S(1)}, u32[]{:S(2)}, u32[]{:S(2)}) collective-permute-start(f32[1,5,2,1,512]{4,3,2,1,0:T(1,128)S(1)} %get-tuple-element.163), channel_id=1, source_target_pairs={{0,1},{1,2},{2,3},{3,4},{4,5},{5,6},{6,7},{7,0},{8,9},{9,10},{10,1... | collective-permute-start | bytes 61448 | tf_op jit(solution)/shard_map/ppermute | solution.py:30
  152.6 11.0 %collective-permute-start.11 = (f32[1,5,2,1,512]{4,3,2,1,0:T(1,128)S(1)}, f32[1,5,2,1,512]{4,3,2,1,0:T(1,128)S(1)}, u32[]{:S(2)}, u32[]{:S(2)}) collective-permute-start(f32[1,5,2,1,512]{4,3,2,1,0:T(1,128)S(1)} %get-tuple-element.164), channel_id=1, source_target_pairs={{1,0},{2,1},{3,2},{4,3},{5,4},{6,5},{7,6},{0,7},{9,8},{10,9},{11,1... | collective-permute-start | bytes 61448 | tf_op jit(solution)/shard_map/ppermute | solution.py:32
  168.4 6.9 %copy-start.81 = (f32[1,5,2,1,512]{4,3,2,1,0:T(1,128)S(1)}, f32[1,5,2,1,512]{4,3,2,1,0:T(1,128)}, u32[]{:S(2)}) copy-start(f32[1,5,2,1,512]{4,3,2,1,0:T(1,128)} %copy-done.80) | copy-start | bytes 61444
  168.4 14.1 %all-to-all-start.4 = ((f32[8,1,10240]{2,1,0:T(1,128)}), f32[8,1,10240]{2,1,0:T(1,128)S(1)}, u32[]{:S(2)}, u32[]{:S(2)}) async-start(f32[8,1,10240]{2,1,0:T(1,128)} %reshape.11904), calls=%async_computation.4 | async-start | bytes 655360 | tf_op jit(solution)/shard_map/all_to_all | solution.py:172
  190.6 14.0 %all-to-all-start.5 = ((f32[8,1,10240]{2,1,0:T(1,128)}), f32[8,1,10240]{2,1,0:T(1,128)S(1)}, u32[]{:S(2)}, u32[]{:S(2)}) async-start(f32[8,1,10240]{2,1,0:T(1,128)} %reshape.11906), calls=%async_computation.5 | async-start | bytes 655360 | tf_op jit(solution)/shard_map/all_to_all | solution.py:175
  195.1 12.0 %collective-permute-start.14 = (f32[1,5,1,32,512]{4,3,2,1,0:T(8,128)}, f32[1,5,1,32,512]{4,3,2,1,0:T(8,128)}, u32[]{:S(2)}, u32[]{:S(2)}) collective-permute-start(f32[1,5,1,32,512]{4,3,2,1,0:T(8,128)} %get-tuple-element.166), channel_id=1, source_target_pairs={{8,0},{9,1},{10,2},{11,3},{12,4},{13,5},{14,6},{15,7},{24,16},{25,... | collective-permute-start | bytes 983048 | tf_op jit(solution)/shard_map/ppermute | solution.py:32
  (136 other events, 159.3 us)
where the time goes:
time: 215 us; the launch traced here: 214 us
  other arithmetic  60.6 us (28%)
  local copies, waits for them, and re-layouts  56.9 us (26%)
  starting transfers between devices  50 us (23%)
  waiting for transfers between devices  40.1 us (19%)
  between operations  5.96 us (3%)
    unnamed x308, local copies, waits for them, and re-layouts  23.2 us
    all_to_all x3, waiting for transfers between devices, rotate_plane(): lax.all_to_all(partner, 'az', split_axis=2, concat_axis=1, tiled=True)  20.5 us
    all_to_all x3, waiting for transfers between devices, rotate_plane(): return lax.all_to_all(rolled, 'az', split_axis=1, concat_axis=2, tiled=True)  19 us
    ppermute x6, starting transfers between devices, padded(): lax.ppermute(head, axis, [((i + 1) % count, i) for i in range(ends)])  14 us
    ppermute x6, starting transfers between devices, padded(): lax.ppermute(tail, axis, [(i, (i + 1) % count) for i in range(ends)])  13.9 us
    div x21, other arithmetic, primitive(): return (vel_theta, vel_radial, vel_axial, press / state[:, 0], press)  11 us
    all_to_all x3, starting transfers between devices, rotate_plane(): return lax.all_to_all(rolled, 'az', split_axis=1, concat_axis=2, tiled=True)  10.9 us
    all_to_all x3, starting transfers between devices, rotate_plane(): lax.all_to_all(partner, 'az', split_axis=2, concat_axis=1, tiled=True)  10.7 us
  transfers between devices with their start and end apart: 21, of which 7 were waited for; matrix products, arithmetic and copies ran while one was open for 43% of the time, Pallas kernels for 0%

commit v1 on v0

--- a/solution.py
+++ b/solution.py
@@ -1,8 +1,11 @@
+import functools
 import math
 
 import jax
 import jax.numpy as jnp
 from jax import lax
+from jax.experimental import pallas as pl
+from jax.experimental.pallas import tpu as pltpu
 from jax.sharding import PartitionSpec as P
 
 HEAT_RATIO = 1.4
@@ -203,6 +206,378 @@
     return state0 / 3.0 + 2.0 / 3.0 * (state2 + TIME_STEP * full_rate(state2, offsets[2]))
 
 
+LANES = 128
+TILE = 8
+PEER = pl.DeviceIdType.MESH
+RUNGE_KUTTA = ((0.0, 1.0), (0.75, 0.25), (1.0 / 3.0, 2.0 / 3.0))
+
+
+def band_of(ax, az, wide):
+    deep, side = az // 2, az % 2
+    column = side + ax * (3 - 2 * side)
+    return column * wide + deep + (column % 2) * (wide - 1 - 2 * deep)
+
+
+def chip_of(band, wide):
+    column, step = band // wide, band % wide
+    ax = column // 2
+    side = (column + ax) % 2
+    deep = step + (column % 2) * (wide - 1 - 2 * step)
+    return ax, deep * 2 + side
+
+
+def kernel(
+    az_count, planes, width,
+    off_ref, den_ref, vel_ref, pre_ref, out_ref,
+    send1, recv1, send2, recv2, base, now, prim, halo_out, halo_in, halo, plane_out, plane_in, ghost,
+    s1, r1, s2, r2, sh, rh, sp, rp,
+):
+    chips = 2 * az_count
+    wide = az_count // 2
+    turn_cells = 32 * az_count
+    tiles = 4
+    row = lax.axis_index("row")
+    ax = lax.axis_index("ax")
+    az = lax.axis_index("az")
+    me = ax * az_count + az
+    band = band_of(ax, az, wide)
+
+    def chip_id(flat):
+        return (row, flat // az_count, flat % az_count)
+
+    def band_id(which):
+        return (row,) + chip_of(which, wide)
+
+    barrier = pltpu.get_barrier_semaphore()
+    for i in range(1, chips):
+        pl.semaphore_signal(barrier, inc=1, device_id=chip_id((me + i) % chips), device_id_type=PEER)
+    pl.semaphore_signal(barrier, inc=1, device_id=(1 - row, ax, az), device_id_type=PEER)
+
+    lane = lax.broadcasted_iota(jnp.int32, (TILE, LANES), 1)
+    part = lane // 32
+    inner = lane % 32
+
+    for f in range(5):
+        for i in range(2):
+            for col in range(4):
+                source = []
+                for h in range(2):
+                    for k in range(2):
+                        rows = pl.ds(16 * h + 8 * i, 8)
+                        cols = pl.ds(128 * col, 128)
+                        if f == 0:
+                            tile = den_ref[0, k, rows, cols]
+                        elif f == 4:
+                            tile = pre_ref[0, k, rows, cols] / den_ref[0, k, rows, cols]
+                        else:
+                            tile = vel_ref[0, f - 1, k, rows, cols]
+                        source.append(tile)
+                for sub in range(4):
+                    mixed = None
+                    for q in range(4):
+                        turn = (32 * (q - sub)) % 128
+                        moved = pltpu.roll(source[q], turn, axis=1) if turn else source[q]
+                        mixed = moved if mixed is None else jnp.where(part == q, moved, mixed)
+                    send1[4 * col + sub, f, 8 * i:8 * i + 8, :] = mixed
+
+    pl.semaphore_wait(barrier, chips)
+
+    def first_copy(i):
+        flat = (me + i) % chips
+        to_ax, to_az = flat // az_count, flat % az_count
+        return pltpu.make_async_remote_copy(
+            src_ref=send1.at[band_of(to_ax, to_az, wide)],
+            dst_ref=recv1.at[me],
+            send_sem=s1.at[i],
+            recv_sem=r1.at[i],
+            device_id=(row, to_ax, to_az),
+            device_id_type=PEER,
+        )
+
+    for i in range(1, chips):
+        first_copy(i).start()
+    recv1[me] = send1[band]
+
+    dtheta = 2.0 * math.pi / turn_cells
+    radius = turn_cells / (2.0 * math.pi) + (band * 32 + inner).astype(jnp.float32) + 0.5
+    inverse = 1.0 / radius
+    c_turn = inverse * (0.5 / dtheta)
+    c_out = 0.5 * (radius + 1.0) * inverse
+    c_in = 0.5 * (radius - 1.0) * inverse
+    l_turn = (inverse * (1.0 / dtheta)) * (inverse * (1.0 / dtheta))
+    l_out = (radius + 0.5) * inverse
+    l_in = (radius - 0.5) * inverse
+    l_mid = 2.0 * l_turn + (2.0 + 2.0 * AXIAL_CURVE)
+    inverse2 = inverse * inverse
+    c_cross = inverse2 * (VISCOSITY / dtheta)
+
+    def pack(w, tile_index, row0, group, slot, packed):
+        low, high = packed
+        low = [jnp.where(inner == tile_index, pltpu.roll(w[f], tile_index + 97, axis=1), low[f]) for f in range(5)]
+        high = [jnp.where(inner == tile_index, pltpu.roll(w[f], tile_index, axis=1), high[f]) for f in range(5)]
+        for f in range(5):
+            moved = pltpu.roll(w[f], (32 * group + 32) % 128, axis=1)
+            rows = pl.ds(pl.multiple_of(row0, 8), 8)
+            plane_out[slot, f, rows, :] = jnp.where(part == group, moved, plane_out[slot, f, rows, :])
+        return low, high
+
+    def close(slot, which, packed):
+        low, high = packed
+        for f in range(5):
+            halo_out[slot, 0, f] = low[f]
+            halo_out[slot, 1, f] = high[f]
+            prim[which, f, 0:8, :] = prim[which, f, turn_cells:turn_cells + 8, :]
+            prim[which, f, turn_cells + 8:turn_cells + 16, :] = prim[which, f, 8:16, :]
+
+    def neighbour_copies(slot):
+        copies = []
+        for side, to in ((0, (band + 1) % chips), (1, (band + chips - 1) % chips)):
+            copies.append(pltpu.make_async_remote_copy(
+                src_ref=halo_out.at[slot, side],
+                dst_ref=halo_in.at[slot, side],
+                send_sem=sh.at[slot, side],
+                recv_sem=rh.at[slot, side],
+                device_id=band_id(to),
+                device_id_type=PEER,
+            ))
+        copies.append(pltpu.make_async_remote_copy(
+            src_ref=plane_out.at[slot],
+            dst_ref=plane_in.at[slot],
+            send_sem=sp.at[slot],
+            recv_sem=rp.at[slot],
+            device_id=(1 - row, ax, az),
+            device_id_type=PEER,
+        ))
+        return copies
+
+    quarter = az_count // 4
+    empty = ([jnp.zeros((TILE, LANES), jnp.float32)] * 5, [jnp.zeros((TILE, LANES), jnp.float32)] * 5)
+
+    for i in range(1, chips):
+        first_copy(i).wait()
+
+    def unpack(a, packed):
+        for t in range(tiles):
+            h, i = t // 2, t % 2
+            w = []
+            for f in range(5):
+                c0 = recv1[a, f, 8 * i:8 * i + 8, :]
+                c1 = recv1[az_count + a, f, 8 * i:8 * i + 8, :]
+                if h == 0:
+                    w.append(jnp.where(part < 2, c0, pltpu.roll(c1, 64, axis=1)))
+                else:
+                    w.append(jnp.where(part < 2, pltpu.roll(c0, 64, axis=1), c1))
+            rho, vt, vr, vz, temp = w
+            rows = pl.ds(pl.multiple_of(a * 32 + t * 8, 8), 8)
+            rows_pad = pl.ds(pl.multiple_of(a * 32 + t * 8 + 8, 8), 8)
+            state = (rho, rho * vt, rho * vr, rho * vz,
+                     rho * (temp / (HEAT_RATIO - 1.0) + 0.5 * (vt * vt + vr * vr + vz * vz)))
+            for f in range(5):
+                base[f, rows, :] = state[f]
+                now[f, rows, :] = state[f]
+                prim[0, f, rows_pad, :] = w[f]
+            packed = pack(w, a * 4 + t, (a % quarter) * 32 + t * 8, a // quarter, 0, packed)
+        return packed
+
+    close(0, 0, lax.fori_loop(0, az_count, unpack, empty))
+
+    def second_copy(flat):
+        return pltpu.make_async_remote_copy(
+            src_ref=send2.at[flat],
+            dst_ref=recv2.at[band],
+            send_sem=s2.at[flat],
+            recv_sem=r2.at[band],
+            device_id=chip_id(flat),
+            device_id_type=PEER,
+        )
+
+    signs = (1.0, -1.0, -1.0, -1.0, 1.0)
+    for step in range(3):
+        copies = neighbour_copies(step)
+        for copy in copies:
+            copy.start()
+        for copy in copies:
+            copy.wait()
+        which = step % 2
+        first_band = band == 0
+        last_band = band == chips - 1
+        for f in range(5):
+            halo[0, f] = jnp.where(first_band, signs[f] * halo_out[step, 1, f], halo_in[step, 0, f])
+            halo[1, f] = jnp.where(last_band, signs[f] * halo_out[step, 0, f], halo_in[step, 1, f])
+        span = 32 * quarter
+        for f in range(5):
+            for g in range(4):
+                moved = plane_in[step, f]
+                if g != 3:
+                    moved = pltpu.roll(moved, 96 - 32 * g, axis=1)
+                if f == 3:
+                    moved = -moved
+                ghost[f, span * g:span * (g + 1), :] = moved
+                ghost[f, turn_cells + span * g:turn_cells + span * (g + 1), :] = moved
+        shift = off_ref[step]
+        shift = jnp.where(row == 0, shift, turn_cells - shift)
+        keep, fresh = RUNGE_KUTTA[step]
+
+        def rate(j, packed, step=step, which=which, shift=shift, keep=keep, fresh=fresh):
+            a = j if step < 2 else (az + j) % az_count
+            result = []
+            for t in range(tiles):
+                tile_index = a * 4 + t
+                row0 = a * 32 + t * 8
+                mid, tl, th, rl, rr, zl, zh = [], [], [], [], [], [], []
+                for f in range(5):
+                    c = prim[which, f, pl.ds(pl.multiple_of(row0 + 8, 8), 8), :]
+                    mid.append(c)
+                    tl.append(prim[which, f, pl.ds(row0 + 7, 8), :])
+                    th.append(prim[which, f, pl.ds(row0 + 9, 8), :])
+                    rl.append(jnp.where(inner == 0, pltpu.roll(halo[0, f], 128 - tile_index, axis=1), pltpu.roll(c, 1, axis=1)))
+                    rr.append(jnp.where(inner == 31, pltpu.roll(halo[1, f], 128 + 31 - tile_index, axis=1), pltpu.roll(c, 127, axis=1)))
+                    zl.append(jnp.where(part == 0, c, pltpu.roll(c, 32, axis=1)))
+                    zh.append(jnp.where(part == 3, ghost[f, pl.ds(row0 + shift, 8), :], pltpu.roll(c, 96, axis=1)))
+
+                def flux(w, d):
+                    rho, vt, vr, vz, temp = w
+                    m = rho * w[1 + d]
+                    terms = [m, m * vt, m * vr, m * vz,
+                             m * (3.5 * temp + 0.5 * (vt * vt + vr * vr + vz * vz))]
+                    terms[1 + d] = terms[1 + d] + rho * temp
+                    return terms
+
+                ftl, fth = flux(tl, 0), flux(th, 0)
+                frl, frh = flux(rl, 1), flux(rr, 1)
+                fzl, fzh = flux(zl, 2), flux(zh, 2)
+                total = [
+                    c_turn * (ftl[f] - fth[f]) + (c_in * frl[f] - c_out * frh[f]) + (fzl[f] - fzh[f])
+                    for f in range(5)
+                ]
+
+                def lap(n):
+                    return (l_turn * (th[n] + tl[n]) + (l_out * rr[n] + l_in * rl[n])
+                            + AXIAL_CURVE * (zh[n] + zl[n]) - l_mid * mid[n])
+
+                rho, vt, vr, vz, temp = mid
+                total[1] = (total[1] - rho * vt * vr * inverse
+                            + VISCOSITY * (lap(1) - vt * inverse2) + c_cross * (th[2] - tl[2]))
+                total[2] = (total[2] + rho * (vt * vt + temp) * inverse
+                            + VISCOSITY * (lap(2) - vr * inverse2) - c_cross * (th[1] - tl[1]))
+                total[3] = total[3] + VISCOSITY * lap(3)
+                total[4] = total[4] + CONDUCTION * lap(4)
+                rows = pl.ds(pl.multiple_of(row0, 8), 8)
+                state = []
+                for f in range(5):
+                    value = fresh * (now[f, rows, :] + TIME_STEP * total[f])
+                    if keep:
+                        value = value + keep * base[f, rows, :]
+                    state.append(value)
+                if step < 2:
+                    inv = 1.0 / state[0]
+                    vt, vr, vz = state[1] * inv, state[2] * inv, state[3] * inv
+                    press = (HEAT_RATIO - 1.0) * (
+                        state[4] - 0.5 * (state[1] * vt + state[2] * vr + state[3] * vz))
+                    w = [state[0], vt, vr, vz, press * inv]
+                    rows_pad = pl.ds(pl.multiple_of(row0 + 8, 8), 8)
+                    for f in range(5):
+                        now[f, rows, :] = state[f]
+                        prim[1 - which, f, rows_pad, :] = w[f]
+                    packed = pack(w, tile_index, (a % quarter) * 32 + t * 8, a // quarter, step + 1, packed)
+                else:
+                    result.append(state)
+            if step == 2:
+                for f in range(5):
+                    for i in range(2):
+                        upper, lower = result[i][f], result[2 + i][f]
+                        send2[a, f, 8 * i:8 * i + 8, :] = jnp.where(part < 2, upper, pltpu.roll(lower, 64, axis=1))
+                        send2[az_count + a, f, 8 * i:8 * i + 8, :] = jnp.where(
+                            part < 2, pltpu.roll(upper, 64, axis=1), lower)
+                for x in range(2):
+                    flat = x * az_count + a
+
+                    @pl.when(flat != me)
+                    def _():
+                        second_copy(flat).start()
+
+                    @pl.when(flat == me)
+                    def _():
+                        recv2[band] = send2[me]
+            return packed
+
+        if step < 2:
+            close(step + 1, 1 - which, lax.fori_loop(0, az_count, rate, empty))
+        else:
+            lax.fori_loop(0, az_count, rate, 0)
+
+    def finish(i, carry):
+        flat = (me + i) % chips
+        from_band = band_of(flat // az_count, flat % az_count, wide)
+        second_copy(flat).wait_send()
+        pltpu.make_async_remote_copy(
+            src_ref=send2.at[flat],
+            dst_ref=recv2.at[from_band],
+            send_sem=s2.at[flat],
+            recv_sem=r2.at[from_band],
+            device_id=chip_id(flat),
+            device_id_type=PEER,
+        ).wait_recv()
+        return carry
+
+    lax.fori_loop(1, chips, finish, 0)
+
+    for f in range(5):
+        for i in range(2):
+            for col in range(4):
+                source = [recv2[4 * col + sub, f, 8 * i:8 * i + 8, :] for sub in range(4)]
+                for q in range(4):
+                    h, k = q // 2, q % 2
+                    mixed = None
+                    for sub in range(4):
+                        turn = (32 * (sub - q)) % 128
+                        moved = pltpu.roll(source[sub], turn, axis=1) if turn else source[sub]
+                        mixed = moved if mixed is None else jnp.where(part == sub, moved, mixed)
+                    out_ref[0, f, k, 16 * h + 8 * i:16 * h + 8 * i + 8, 128 * col:128 * col + 128] = mixed
+
+
+def banded(az_count, density, velocity, pressure, offsets):
+    chips = 2 * az_count
+    cells = 32 * az_count
+    planes, width = 4, 32
+    f32 = jnp.float32
+    dma = pltpu.SemaphoreType.DMA
+    vmem = pl.BlockSpec(memory_space=pltpu.VMEM)
+    return pl.pallas_call(
+        functools.partial(kernel, az_count, planes, width),
+        out_shape=jax.ShapeDtypeStruct((1, 5) + density.shape[1:], f32),
+        in_specs=[pl.BlockSpec(memory_space=pltpu.SMEM), vmem, vmem, vmem],
+        out_specs=vmem,
+        scratch_shapes=[
+            pltpu.VMEM((chips, 5, 16, LANES), f32),
+            pltpu.VMEM((chips, 5, 16, LANES), f32),
+            pltpu.VMEM((chips, 5, 16, LANES), f32),
+            pltpu.VMEM((chips, 5, 16, LANES), f32),
+            pltpu.VMEM((5, cells, LANES), f32),
+            pltpu.VMEM((5, cells, LANES), f32),
+            pltpu.VMEM((2, 5, cells + 16, LANES), f32),
+            pltpu.VMEM((3, 2, 5, TILE, LANES), f32),
+            pltpu.VMEM((3, 2, 5, TILE, LANES), f32),
+            pltpu.VMEM((2, 5, TILE, LANES), f32),
+            pltpu.VMEM((3, 5, cells // 4, LANES), f32),
+            pltpu.VMEM((3, 5, cells // 4, LANES), f32),
+            pltpu.VMEM((5, 2 * cells + 8, LANES), f32),
+            dma((chips,)), dma((chips,)), dma((chips,)), dma((chips,)),
+            dma((3, 2)), dma((3, 2)), dma((3,)), dma((3,)),
+        ],
+        compiler_params=pltpu.CompilerParams(
+            collective_id=0, has_side_effects=True, vmem_limit_bytes=40 * 2**20
+        ),
+    )(offsets, density, velocity, pressure)
+
+
+def whole_step(density, velocity, pressure, offsets):
+    ax_count, az_count = lax.axis_size("ax"), lax.axis_size("az")
+    if ax_count == 2 and az_count == 8 and density.shape == (1, 2, 32, 512):
+        return banded(az_count, density, velocity, pressure, offsets)
+    return body(density, velocity, pressure, offsets)
+
+
 def solution(mesh):
     placed = (
         P("row", "ax", "az", None),
@@ -211,7 +586,7 @@
         P(),
     )
     return jax.shard_map(
-        body,
+        whole_step,
         mesh=mesh,
         in_specs=placed,
         out_specs=P("row", None, "ax", "az", None),

time: 215 us -> 60.2 us (0.28)
  the two profiles are of different devices: /device:TPU:0 before, /device:TPU:14 now
where the time goes in v1:
time: 60.2 us; the launch traced here: 60.1 us
  Pallas kernels  55.8 us (93%)
  local copies, waits for them, and re-layouts  4.3 us (7%)
    pallas_call x1, Pallas kernels, banded(): pl.pallas_call(functools.partial(kernel, az_count, planes, width), out_sh...  55.8 us
    unnamed x9, local copies, waits for them, and re-layouts  4.3 us

profile of v1, /device:TPU:14, one launch (start us, length us, event | category | flops | bytes accessed | tf_op | source)
XLA Modules:
  0.0 60.1 jit_solution(12941899654568500814)
XLA Ops:
  0.0 0.0 copy-start
  0.0 1.0 %copy-done = f32[1,3,2,32,512]{4,3,2,1,0:T(8,128)S(1)} copy-done((f32[1,3,2,32,512]{4,3,2,1,0:T(8,128)S(1)}, f32[1,3,2,32,512]{4,3,2,1,0:T(8,128)}, u32[]{:S(2)}) %copy-start) | copy-done | bytes 393240
  1.0 0.0 copy-start.1
  1.0 0.9 %copy-done.1 = f32[1,2,32,512]{3,2,1,0:T(8,128)S(1)} copy-done((f32[1,2,32,512]{3,2,1,0:T(8,128)S(1)}, f32[1,2,32,512]{3,2,1,0:T(8,128)}, u32[]{:S(2)}) %copy-start.1) | copy-done | bytes 131096
  1.9 0.0 copy-start.2
  1.9 0.9 %copy-done.2 = f32[1,2,32,512]{3,2,1,0:T(8,128)S(1)} copy-done((f32[1,2,32,512]{3,2,1,0:T(8,128)S(1)}, f32[1,2,32,512]{3,2,1,0:T(8,128)}, u32[]{:S(2)}) %copy-start.2) | copy-done | bytes 131096
  2.8 0.0 copy-start.3
  2.8 0.7 %copy-done.3 = s32[3]{0:T(128)S(1)} copy-done((s32[3]{0:T(128)S(1)}, s32[3]{0:T(128)}, u32[]{:S(2)}) %copy-start.3) | copy-done | bytes 36
  3.5 55.8 %shard_map.46 = f32[1,5,2,32,512]{4,3,2,1,0:T(8,128)S(1)} custom-call(s32[3]{0:T(128)S(1)} %copy-done.3, f32[1,2,32,512]{3,2,1,0:T(8,128)S(1)} %copy-done.1, f32[1,3,2,32,512]{4,3,2,1,0:T(8,128)S(1)} %copy-done, f32[1,2,32,512]{3,2,1,0:T(8,128)S(1)} %copy-done.2), custom_call_target="tpu_custom_call" | custom-call | tf_op jit(solution)/shard_map/pallas_call | solution.py:546
  59.2 0.8 %copy.6 = f32[1,5,2,32,512]{4,3,2,1,0:T(8,128)} copy(f32[1,5,2,32,512]{4,3,2,1,0:T(8,128)S(1)} %shard_map.46) | data formatting | bytes 1310720
Async XLA Ops:
  0.0 1.0 %copy-start = (f32[1,3,2,32,512]{4,3,2,1,0:T(8,128)S(1)}, f32[1,3,2,32,512]{4,3,2,1,0:T(8,128)}, u32[]{:S(2)}) copy-start(f32[1,3,2,32,512]{4,3,2,1,0:T(8,128)} %vel_ref.1) | copy-start | bytes 1179652
  1.0 0.9 %copy-start.1 = (f32[1,2,32,512]{3,2,1,0:T(8,128)S(1)}, f32[1,2,32,512]{3,2,1,0:T(8,128)}, u32[]{:S(2)}) copy-start(f32[1,2,32,512]{3,2,1,0:T(8,128)} %den_ref.1) | copy-start | bytes 393220
  1.9 0.9 %copy-start.2 = (f32[1,2,32,512]{3,2,1,0:T(8,128)S(1)}, f32[1,2,32,512]{3,2,1,0:T(8,128)}, u32[]{:S(2)}) copy-start(f32[1,2,32,512]{3,2,1,0:T(8,128)} %pre_ref.1) | copy-start | bytes 393220
  2.8 0.7 %copy-start.3 = (s32[3]{0:T(128)S(1)}, s32[3]{0:T(128)}, u32[]{:S(2)}) copy-start(s32[3]{0:T(128)} %off_ref.1) | copy-start | bytes 40

commit v2 on v1

--- a/solution.py
+++ b/solution.py
@@ -227,10 +227,11 @@
 
 
 def kernel(
-    az_count, planes, width,
+    az_count,
+    off_hbm, den_hbm, vel_hbm, pre_hbm, out_hbm,
     off_ref, den_ref, vel_ref, pre_ref, out_ref,
     send1, recv1, send2, recv2, base, now, prim, halo_out, halo_in, halo, plane_out, plane_in, ghost,
-    s1, r1, s2, r2, sh, rh, sp, rp,
+    s1, r1, s2, r2, sh, rh, sp, rp, s_in, s_out,
 ):
     chips = 2 * az_count
     wide = az_count // 2
@@ -248,6 +249,13 @@
     def band_id(which):
         return (row,) + chip_of(which, wide)
 
+    loads = [
+        pltpu.make_async_copy(src, dst, s_in.at[n])
+        for n, (src, dst) in enumerate((
+            (den_hbm, den_ref), (pre_hbm, pre_ref), (vel_hbm, vel_ref), (off_hbm, off_ref)))
+    ]
+    for load in loads:
+        load.start()
     barrier = pltpu.get_barrier_semaphore()
     for i in range(1, chips):
         pl.semaphore_signal(barrier, inc=1, device_id=chip_id((me + i) % chips), device_id_type=PEER)
@@ -256,6 +264,9 @@
     lane = lax.broadcasted_iota(jnp.int32, (TILE, LANES), 1)
     part = lane // 32
     inner = lane % 32
+
+    for load in loads:
+        load.wait()
 
     for f in range(5):
         for i in range(2):
@@ -282,20 +293,24 @@
 
     pl.semaphore_wait(barrier, chips)
 
-    def first_copy(i):
-        flat = (me + i) % chips
-        to_ax, to_az = flat // az_count, flat % az_count
+    def first_copy(flat):
         return pltpu.make_async_remote_copy(
-            src_ref=send1.at[band_of(to_ax, to_az, wide)],
+            src_ref=send1.at[band_of(flat // az_count, flat % az_count, wide)],
             dst_ref=recv1.at[me],
-            send_sem=s1.at[i],
-            recv_sem=r1.at[i],
-            device_id=(row, to_ax, to_az),
+            send_sem=s1.at[flat],
+            recv_sem=r1.at[me],
+            device_id=chip_id(flat),
             device_id_type=PEER,
         )
 
-    for i in range(1, chips):
-        first_copy(i).start()
+    def others():
+        for j in range(az_count):
+            for x in range(2):
+                if j or x:
+                    yield ((ax + x) % 2) * az_count + (az + az_count - j) % az_count
+
+    for flat in others():
+        first_copy(flat).start()
     recv1[me] = send1[band]
 
     dtheta = 2.0 * math.pi / turn_cells
@@ -310,24 +325,39 @@
     l_mid = 2.0 * l_turn + (2.0 + 2.0 * AXIAL_CURVE)
     inverse2 = inverse * inverse
     c_cross = inverse2 * (VISCOSITY / dtheta)
-
-    def pack(w, tile_index, row0, group, slot, packed):
-        low, high = packed
-        low = [jnp.where(inner == tile_index, pltpu.roll(w[f], tile_index + 97, axis=1), low[f]) for f in range(5)]
-        high = [jnp.where(inner == tile_index, pltpu.roll(w[f], tile_index, axis=1), high[f]) for f in range(5)]
+    r_low = turn_cells / (2.0 * math.pi) + (lane * 0 + band * 32).astype(jnp.float32) + 0.5
+    r_high = r_low + 31.0
+    edge_c = (0.5 * (r_low - 1.0) / r_low, -0.5 * (r_high + 1.0) / r_high)
+    edge_l = ((r_low - 0.5) / r_low, (r_high + 0.5) / r_high)
+    zero = jnp.zeros((TILE, LANES), jnp.float32)
+    c_in = jnp.where(inner == 0, zero, c_in)
+    l_in = jnp.where(inner == 0, zero, l_in)
+    c_out = jnp.where(inner == 31, zero, c_out)
+    l_out = jnp.where(inner == 31, zero, l_out)
+
+    def pack(tiles_of, a, slot):
+        group = a // quarter
         for f in range(5):
-            moved = pltpu.roll(w[f], (32 * group + 32) % 128, axis=1)
-            rows = pl.ds(pl.multiple_of(row0, 8), 8)
-            plane_out[slot, f, rows, :] = jnp.where(part == group, moved, plane_out[slot, f, rows, :])
-        return low, high
-
-    def close(slot, which, packed):
-        low, high = packed
-        for f in range(5):
-            halo_out[slot, 0, f] = low[f]
-            halo_out[slot, 1, f] = high[f]
-            prim[which, f, 0:8, :] = prim[which, f, turn_cells:turn_cells + 8, :]
-            prim[which, f, turn_cells + 8:turn_cells + 16, :] = prim[which, f, 8:16, :]
+            low, high = halo_out[slot, 0, f], halo_out[slot, 1, f]
+            for t in range(tiles):
+                w, tile_index = tiles_of[t][f], a * 4 + t
+                low = jnp.where(inner == tile_index, pltpu.roll(w, tile_index + 97, axis=1), low)
+                high = jnp.where(inner == tile_index, pltpu.roll(w, tile_index, axis=1), high)
+                moved = pltpu.roll(w, (32 * group + 32) % 128, axis=1)
+                rows = pl.ds(pl.multiple_of((a % quarter) * 32 + t * 8, 8), 8)
+                plane_out[slot, f, rows, :] = jnp.where(part == group, moved, plane_out[slot, f, rows, :])
+            halo_out[slot, 0, f], halo_out[slot, 1, f] = low, high
+
+    def wrap(which, a, tiles_of):
+        @pl.when(a == 0)
+        def _():
+            for f in range(5):
+                prim[which, f, turn_cells + 8:turn_cells + 16, :] = tiles_of[0][f]
+
+        @pl.when(a == az_count - 1)
+        def _():
+            for f in range(5):
+                prim[which, f, 0:8, :] = tiles_of[tiles - 1][f]
 
     def neighbour_copies(slot):
         copies = []
@@ -351,12 +381,59 @@
         return copies
 
     quarter = az_count // 4
-    empty = ([jnp.zeros((TILE, LANES), jnp.float32)] * 5, [jnp.zeros((TILE, LANES), jnp.float32)] * 5)
-
-    for i in range(1, chips):
-        first_copy(i).wait()
-
-    def unpack(a, packed):
+    drag = (0.0, VISCOSITY, VISCOSITY, VISCOSITY, CONDUCTION)
+
+    def flux(w, d):
+        rho, vt, vr, vz, temp = w
+        m = rho * w[1 + d]
+        terms = [m, m * vt, m * vr, m * vz,
+                 m * (3.5 * temp + 0.5 * (vt * vt + vr * vr + vz * vz))]
+        terms[1 + d] = terms[1 + d] + rho * temp
+        return terms
+
+    def inside(a, step):
+        which = step % 2
+        keep, fresh = RUNGE_KUTTA[step]
+        for t in range(tiles):
+            row0 = a * 32 + t * 8
+            mid, tl, th, rl, rr, zl, zh = [], [], [], [], [], [], []
+            for f in range(5):
+                c = prim[which, f, pl.ds(pl.multiple_of(row0 + 8, 8), 8), :]
+                mid.append(c)
+                tl.append(prim[which, f, pl.ds(row0 + 7, 8), :])
+                th.append(prim[which, f, pl.ds(row0 + 9, 8), :])
+                rl.append(pltpu.roll(c, 1, axis=1))
+                rr.append(pltpu.roll(c, 127, axis=1))
+                zl.append(jnp.where(part == 0, c, pltpu.roll(c, 32, axis=1)))
+                zh.append(jnp.where(part == 3, zero, pltpu.roll(c, 96, axis=1)))
+            ftl, fth = flux(tl, 0), flux(th, 0)
+            frl, frh = flux(rl, 1), flux(rr, 1)
+            fzl, fzh = flux(zl, 2), flux(zh, 2)
+            total = [
+                c_turn * (ftl[f] - fth[f]) + (c_in * frl[f] - c_out * frh[f]) + (fzl[f] - fzh[f])
+                for f in range(5)
+            ]
+
+            def lap(n):
+                return (l_turn * (th[n] + tl[n]) + (l_out * rr[n] + l_in * rl[n])
+                        + AXIAL_CURVE * (zh[n] + zl[n]) - l_mid * mid[n])
+
+            rho, vt, vr, vz, temp = mid
+            total[1] = (total[1] - rho * vt * vr * inverse
+                        + VISCOSITY * (lap(1) - vt * inverse2) + c_cross * (th[2] - tl[2]))
+            total[2] = (total[2] + rho * (vt * vt + temp) * inverse
+                        + VISCOSITY * (lap(2) - vr * inverse2) - c_cross * (th[1] - tl[1]))
+            total[3] = total[3] + VISCOSITY * lap(3)
+            total[4] = total[4] + CONDUCTION * lap(4)
+            rows = pl.ds(pl.multiple_of(row0, 8), 8)
+            for f in range(5):
+                value = fresh * (now[f, rows, :] + TIME_STEP * total[f])
+                if keep:
+                    value = value + keep * base[f, rows, :]
+                now[f, rows, :] = value
+
+    def unpack(a):
+        tiles_of = []
         for t in range(tiles):
             h, i = t // 2, t % 2
             w = []
@@ -376,10 +453,35 @@
                 base[f, rows, :] = state[f]
                 now[f, rows, :] = state[f]
                 prim[0, f, rows_pad, :] = w[f]
-            packed = pack(w, a * 4 + t, (a % quarter) * 32 + t * 8, a // quarter, 0, packed)
-        return packed
-
-    close(0, 0, lax.fori_loop(0, az_count, unpack, empty))
+            tiles_of.append(w)
+        wrap(0, a, tiles_of)
+        pack(tiles_of, a, 0)
+
+    def arrive(j, carry):
+        a = (az + j) % az_count
+        for x in range(2):
+            flat = x * az_count + a
+
+            @pl.when(flat != me)
+            def _():
+                pltpu.make_async_remote_copy(
+                    src_ref=send1.at[flat],
+                    dst_ref=recv1.at[flat],
+                    send_sem=s1.at[flat],
+                    recv_sem=r1.at[flat],
+                    device_id=chip_id(flat),
+                    device_id_type=PEER,
+                ).wait_recv()
+
+        unpack(a)
+
+        @pl.when(j >= 2)
+        def _():
+            inside((a + az_count - 1) % az_count, 0)
+
+        return carry
+
+    lax.fori_loop(0, az_count, arrive, 0)
 
     def second_copy(flat):
         return pltpu.make_async_remote_copy(
@@ -396,79 +498,70 @@
         copies = neighbour_copies(step)
         for copy in copies:
             copy.start()
+        if step == 0:
+            def rest(j, carry):
+                inside((az + az_count - 1 + j) % az_count, 0)
+                return carry
+
+            lax.fori_loop(0, 2, rest, 0)
+        else:
+            def sweep(a, carry, step=step):
+                inside(a, step)
+                return carry
+
+            lax.fori_loop(0, az_count, sweep, 0)
         for copy in copies:
             copy.wait()
-        which = step % 2
-        first_band = band == 0
-        last_band = band == chips - 1
-        for f in range(5):
-            halo[0, f] = jnp.where(first_band, signs[f] * halo_out[step, 1, f], halo_in[step, 0, f])
-            halo[1, f] = jnp.where(last_band, signs[f] * halo_out[step, 0, f], halo_in[step, 1, f])
-        span = 32 * quarter
-        for f in range(5):
-            for g in range(4):
-                moved = plane_in[step, f]
-                if g != 3:
-                    moved = pltpu.roll(moved, 96 - 32 * g, axis=1)
-                if f == 3:
-                    moved = -moved
-                ghost[f, span * g:span * (g + 1), :] = moved
-                ghost[f, turn_cells + span * g:turn_cells + span * (g + 1), :] = moved
+        weight = TIME_STEP * RUNGE_KUTTA[step][1]
+        walls = (band == 0, band == chips - 1)
+        for side in range(2):
+            w = [
+                jnp.where(walls[side], signs[f] * halo_out[step, 1 - side, f], halo_in[step, side, f])
+                for f in range(5)
+            ]
+            terms = flux(w, 1)
+            for f in range(5):
+                value = edge_c[side] * terms[f]
+                if f:
+                    value = value + drag[f] * edge_l[side] * w[f]
+                halo[side, f] = weight * value
+
+        def slide(n, carry, step=step, weight=weight):
+            rows = pl.ds(pl.multiple_of(n * 8, 8), 8)
+            w = [plane_in[step, f, rows, :] for f in range(5)]
+            w[3] = -w[3]
+            terms = flux(w, 2)
+            for f in range(5):
+                value = -terms[f]
+                if f:
+                    value = value + (AXIAL_CURVE * drag[f]) * w[f]
+                value = weight * value
+                for g in range(4):
+                    moved = pltpu.roll(value, 96 - 32 * g, axis=1) if g != 3 else value
+                    place = 32 * quarter * g + n * 8
+                    ghost[f, pl.ds(pl.multiple_of(place, 8), 8), :] = moved
+                    ghost[f, pl.ds(pl.multiple_of(turn_cells + place, 8), 8), :] = moved
+            return carry
+
+        lax.fori_loop(0, 4 * quarter, slide, 0)
         shift = off_ref[step]
         shift = jnp.where(row == 0, shift, turn_cells - shift)
-        keep, fresh = RUNGE_KUTTA[step]
-
-        def rate(j, packed, step=step, which=which, shift=shift, keep=keep, fresh=fresh):
+
+        def edges(j, carry, step=step, shift=shift):
+            which = step % 2
             a = j if step < 2 else (az + j) % az_count
-            result = []
+            states, prims = [], []
             for t in range(tiles):
                 tile_index = a * 4 + t
                 row0 = a * 32 + t * 8
-                mid, tl, th, rl, rr, zl, zh = [], [], [], [], [], [], []
-                for f in range(5):
-                    c = prim[which, f, pl.ds(pl.multiple_of(row0 + 8, 8), 8), :]
-                    mid.append(c)
-                    tl.append(prim[which, f, pl.ds(row0 + 7, 8), :])
-                    th.append(prim[which, f, pl.ds(row0 + 9, 8), :])
-                    rl.append(jnp.where(inner == 0, pltpu.roll(halo[0, f], 128 - tile_index, axis=1), pltpu.roll(c, 1, axis=1)))
-                    rr.append(jnp.where(inner == 31, pltpu.roll(halo[1, f], 128 + 31 - tile_index, axis=1), pltpu.roll(c, 127, axis=1)))
-                    zl.append(jnp.where(part == 0, c, pltpu.roll(c, 32, axis=1)))
-                    zh.append(jnp.where(part == 3, ghost[f, pl.ds(row0 + shift, 8), :], pltpu.roll(c, 96, axis=1)))
-
-                def flux(w, d):
-                    rho, vt, vr, vz, temp = w
-                    m = rho * w[1 + d]
-                    terms = [m, m * vt, m * vr, m * vz,
-                             m * (3.5 * temp + 0.5 * (vt * vt + vr * vr + vz * vz))]
-                    terms[1 + d] = terms[1 + d] + rho * temp
-                    return terms
-
-                ftl, fth = flux(tl, 0), flux(th, 0)
-                frl, frh = flux(rl, 1), flux(rr, 1)
-                fzl, fzh = flux(zl, 2), flux(zh, 2)
-                total = [
-                    c_turn * (ftl[f] - fth[f]) + (c_in * frl[f] - c_out * frh[f]) + (fzl[f] - fzh[f])
-                    for f in range(5)
-                ]
-
-                def lap(n):
-                    return (l_turn * (th[n] + tl[n]) + (l_out * rr[n] + l_in * rl[n])
-                            + AXIAL_CURVE * (zh[n] + zl[n]) - l_mid * mid[n])
-
-                rho, vt, vr, vz, temp = mid
-                total[1] = (total[1] - rho * vt * vr * inverse
-                            + VISCOSITY * (lap(1) - vt * inverse2) + c_cross * (th[2] - tl[2]))
-                total[2] = (total[2] + rho * (vt * vt + temp) * inverse
-                            + VISCOSITY * (lap(2) - vr * inverse2) - c_cross * (th[1] - tl[1]))
-                total[3] = total[3] + VISCOSITY * lap(3)
-                total[4] = total[4] + CONDUCTION * lap(4)
                 rows = pl.ds(pl.multiple_of(row0, 8), 8)
                 state = []
                 for f in range(5):
-                    value = fresh * (now[f, rows, :] + TIME_STEP * total[f])
-                    if keep:
-                        value = value + keep * base[f, rows, :]
-                    state.append(value)
+                    low = pltpu.roll(halo[0, f], 128 - tile_index, axis=1)
+                    high = pltpu.roll(halo[1, f], 128 + 31 - tile_index, axis=1)
+                    extra = jnp.where(inner == 0, low, jnp.where(inner == 31, high, zero))
+                    extra = extra + jnp.where(part == 3, ghost[f, pl.ds(row0 + shift, 8), :], zero)
+                    state.append(now[f, rows, :] + extra)
                 if step < 2:
                     inv = 1.0 / state[0]
                     vt, vr, vz = state[1] * inv, state[2] * inv, state[3] * inv
@@ -479,52 +572,53 @@
                     for f in range(5):
                         now[f, rows, :] = state[f]
                         prim[1 - which, f, rows_pad, :] = w[f]
-                    packed = pack(w, tile_index, (a % quarter) * 32 + t * 8, a // quarter, step + 1, packed)
+                    prims.append(w)
                 else:
-                    result.append(state)
-            if step == 2:
-                for f in range(5):
-                    for i in range(2):
-                        upper, lower = result[i][f], result[2 + i][f]
-                        send2[a, f, 8 * i:8 * i + 8, :] = jnp.where(part < 2, upper, pltpu.roll(lower, 64, axis=1))
-                        send2[az_count + a, f, 8 * i:8 * i + 8, :] = jnp.where(
-                            part < 2, pltpu.roll(upper, 64, axis=1), lower)
-                for x in range(2):
-                    flat = x * az_count + a
-
-                    @pl.when(flat != me)
-                    def _():
-                        second_copy(flat).start()
-
-                    @pl.when(flat == me)
-                    def _():
-                        recv2[band] = send2[me]
-            return packed
-
-        if step < 2:
-            close(step + 1, 1 - which, lax.fori_loop(0, az_count, rate, empty))
-        else:
-            lax.fori_loop(0, az_count, rate, 0)
-
-    def finish(i, carry):
-        flat = (me + i) % chips
-        from_band = band_of(flat // az_count, flat % az_count, wide)
-        second_copy(flat).wait_send()
-        pltpu.make_async_remote_copy(
-            src_ref=send2.at[flat],
-            dst_ref=recv2.at[from_band],
-            send_sem=s2.at[flat],
-            recv_sem=r2.at[from_band],
-            device_id=chip_id(flat),
-            device_id_type=PEER,
-        ).wait_recv()
-        return carry
-
-    lax.fori_loop(1, chips, finish, 0)
-
-    for f in range(5):
-        for i in range(2):
-            for col in range(4):
+                    states.append(state)
+            if step < 2:
+                wrap(1 - which, a, prims)
+                pack(prims, a, step + 1)
+                return carry
+            for f in range(5):
+                for i in range(2):
+                    upper, lower = states[i][f], states[2 + i][f]
+                    send2[a, f, 8 * i:8 * i + 8, :] = jnp.where(part < 2, upper, pltpu.roll(lower, 64, axis=1))
+                    send2[az_count + a, f, 8 * i:8 * i + 8, :] = jnp.where(
+                        part < 2, pltpu.roll(upper, 64, axis=1), lower)
+            for x in range(2):
+                flat = x * az_count + a
+
+                @pl.when(flat != me)
+                def _():
+                    second_copy(flat).start()
+
+                @pl.when(flat == me)
+                def _():
+                    recv2[band] = send2[me]
+            return carry
+
+        lax.fori_loop(0, az_count, edges, 0)
+
+    stores = []
+    for col in range(4):
+        for sub in range(4):
+            from_band = 4 * col + sub
+            from_ax, from_az = chip_of(from_band, wide)
+            flat = from_ax * az_count + from_az
+
+            @pl.when(flat != me)
+            def _():
+                pltpu.make_async_remote_copy(
+                    src_ref=send2.at[flat],
+                    dst_ref=recv2.at[from_band],
+                    send_sem=s2.at[flat],
+                    recv_sem=r2.at[from_band],
+                    device_id=chip_id(flat),
+                    device_id_type=PEER,
+                ).wait_recv()
+
+        for f in range(5):
+            for i in range(2):
                 source = [recv2[4 * col + sub, f, 8 * i:8 * i + 8, :] for sub in range(4)]
                 for q in range(4):
                     h, k = q // 2, q % 2
@@ -533,22 +627,36 @@
                         turn = (32 * (sub - q)) % 128
                         moved = pltpu.roll(source[sub], turn, axis=1) if turn else source[sub]
                         mixed = moved if mixed is None else jnp.where(part == sub, moved, mixed)
-                    out_ref[0, f, k, 16 * h + 8 * i:16 * h + 8 * i + 8, 128 * col:128 * col + 128] = mixed
+                    out_ref[col, f, k, 16 * h + 8 * i:16 * h + 8 * i + 8, :] = mixed
+        store = pltpu.make_async_copy(
+            out_ref.at[col], out_hbm.at[0, :, :, :, pl.ds(128 * col, 128)], s_out.at[col])
+        store.start()
+        stores.append(store)
+
+    for flat in others():
+        first_copy(flat).wait_send()
+        second_copy(flat).wait_send()
+    for store in stores:
+        store.wait()
 
 
 def banded(az_count, density, velocity, pressure, offsets):
     chips = 2 * az_count
     cells = 32 * az_count
-    planes, width = 4, 32
     f32 = jnp.float32
     dma = pltpu.SemaphoreType.DMA
-    vmem = pl.BlockSpec(memory_space=pltpu.VMEM)
+    anywhere = pl.BlockSpec(memory_space=pl.ANY)
     return pl.pallas_call(
-        functools.partial(kernel, az_count, planes, width),
+        functools.partial(kernel, az_count),
         out_shape=jax.ShapeDtypeStruct((1, 5) + density.shape[1:], f32),
-        in_specs=[pl.BlockSpec(memory_space=pltpu.SMEM), vmem, vmem, vmem],
-        out_specs=vmem,
+        in_specs=[anywhere] * 4,
+        out_specs=anywhere,
         scratch_shapes=[
+            pltpu.SMEM(offsets.shape, jnp.int32),
+            pltpu.VMEM(density.shape, f32),
+            pltpu.VMEM(velocity.shape, f32),
+            pltpu.VMEM(pressure.shape, f32),
+            pltpu.VMEM((4, 5, 2, 32, LANES), f32),
             pltpu.VMEM((chips, 5, 16, LANES), f32),
             pltpu.VMEM((chips, 5, 16, LANES), f32),
             pltpu.VMEM((chips, 5, 16, LANES), f32),
@@ -563,10 +671,10 @@
             pltpu.VMEM((3, 5, cells // 4, LANES), f32),
             pltpu.VMEM((5, 2 * cells + 8, LANES), f32),
             dma((chips,)), dma((chips,)), dma((chips,)), dma((chips,)),
-            dma((3, 2)), dma((3, 2)), dma((3,)), dma((3,)),
+            dma((3, 2)), dma((3, 2)), dma((3,)), dma((3,)), dma((4,)), dma((4,)),
         ],
         compiler_params=pltpu.CompilerParams(
-            collective_id=0, has_side_effects=True, vmem_limit_bytes=40 * 2**20
+            collective_id=0, has_side_effects=True, vmem_limit_bytes=56 * 2**20
         ),
     )(offsets, density, velocity, pressure)
 

time: 60.2 us -> 56.3 us (0.935)
  local copies, waits for them, and re-layouts: 4.3 us -> 1.97 us
  Pallas kernels: 55.8 us -> 54.1 us
    unnamed x9 -> x1, local copies, waits for them, and re-layouts: 4.3 us -> 1.97 us
    pallas_call x1, Pallas kernels: 55.8 us -> 54.1 us  [banded(): pl.pallas_call(functools.partial(kernel, az_count), out_shape=jax.ShapeDt...]
where the time goes in v2:
time: 56.3 us; the launch traced here: 56.1 us
  Pallas kernels  54.1 us (96%)
  local copies, waits for them, and re-layouts  1.97 us (3%)
    pallas_call x1, Pallas kernels, banded(): pl.pallas_call(functools.partial(kernel, az_count), out_shape=jax.ShapeDt...  54.1 us
    unnamed x1, local copies, waits for them, and re-layouts  1.97 us

profile of v2, /device:TPU:14, one launch (start us, length us, event | category | flops | bytes accessed | tf_op | source)
XLA Modules:
  0.0 56.1 jit_solution(5328564508840252528)
XLA Ops:
  0.0 54.1 %shard_map.46 = f32[1,5,2,32,512]{4,3,2,1,0:T(8,128)} custom-call(s32[3]{0:T(128)} %off_hbm.1, f32[1,2,32,512]{3,2,1,0:T(8,128)} %den_hbm.1, f32[1,3,2,32,512]{4,3,2,1,0:T(8,128)} %vel_hbm.1, f32[1,2,32,512]{3,2,1,0:T(8,128)} %pre_hbm.1), custom_call_target="tpu_custom_call" | custom-call | tf_op jit(solution)/shard_map/pallas_call | solution.py:649
  54.1 2.0 %copy.6 = f32[1,5,2,32,512]{4,3,2,1,0:T(8,128)} copy(f32[1,5,2,32,512]{4,3,2,1,0:T(8,128)} %shard_map.46) | data formatting | bytes 1310720

commit v3 on v2

--- a/solution.py
+++ b/solution.py
@@ -226,14 +226,19 @@
     return ax, deep * 2 + side
 
 
+def spread(j, half):
+    return half + (j % 2) * ((j + 1) // 2) - (1 - j % 2) * (j // 2)
+
+
 def kernel(
     az_count,
-    off_hbm, den_hbm, vel_hbm, pre_hbm, out_hbm,
-    off_ref, den_ref, vel_ref, pre_ref, out_ref,
+    off_hbm, den_hbm, vel_hbm, pre_hbm, out_ref,
+    off_ref, den_ref, vel_ref, pre_ref,
     send1, recv1, send2, recv2, base, now, prim, halo_out, halo_in, halo, plane_out, plane_in, ghost,
-    s1, r1, s2, r2, sh, rh, sp, rp, s_in, s_out,
+    s1, r1, s2, r2, sh, rh, sp, rp, s_in,
 ):
     chips = 2 * az_count
+    half = az_count // 2
     wide = az_count // 2
     turn_cells = 32 * az_count
     tiles = 4
@@ -306,8 +311,9 @@
     def others():
         for j in range(az_count):
             for x in range(2):
-                if j or x:
-                    yield ((ax + x) % 2) * az_count + (az + az_count - j) % az_count
+                offset = spread(j, half) % az_count
+                if offset or x:
+                    yield ((ax + x) % 2) * az_count + (az + az_count - offset) % az_count
 
     for flat in others():
         first_copy(flat).start()
@@ -458,7 +464,7 @@
         pack(tiles_of, a, 0)
 
     def arrive(j, carry):
-        a = (az + j) % az_count
+        a = (az + spread(j, half)) % az_count
         for x in range(2):
             flat = x * az_count + a
 
@@ -477,7 +483,7 @@
 
         @pl.when(j >= 2)
         def _():
-            inside((a + az_count - 1) % az_count, 0)
+            inside((az + spread(j - 2, half)) % az_count, 0)
 
         return carry
 
@@ -500,16 +506,16 @@
             copy.start()
         if step == 0:
             def rest(j, carry):
-                inside((az + az_count - 1 + j) % az_count, 0)
+                inside((az + spread(j + az_count - 2, half)) % az_count, 0)
                 return carry
 
             lax.fori_loop(0, 2, rest, 0)
         else:
             def sweep(a, carry, step=step):
-                inside(a, step)
+                inside((az + spread(a, half)) % az_count, step)
                 return carry
 
-            lax.fori_loop(0, az_count, sweep, 0)
+            lax.fori_loop(0, az_count if step == 1 else half, sweep, 0)
         for copy in copies:
             copy.wait()
         weight = TIME_STEP * RUNGE_KUTTA[step][1]
@@ -549,7 +555,12 @@
 
         def edges(j, carry, step=step, shift=shift):
             which = step % 2
-            a = j if step < 2 else (az + j) % az_count
+            a = j if step < 2 else (az + spread(j, half)) % az_count
+            if step == 2:
+                @pl.when(j >= half)
+                def _():
+                    inside(a, step)
+
             states, prims = [], []
             for t in range(tiles):
                 tile_index = a * 4 + t
@@ -599,7 +610,6 @@
 
         lax.fori_loop(0, az_count, edges, 0)
 
-    stores = []
     for col in range(4):
         for sub in range(4):
             from_band = 4 * col + sub
@@ -627,17 +637,11 @@
                         turn = (32 * (sub - q)) % 128
                         moved = pltpu.roll(source[sub], turn, axis=1) if turn else source[sub]
                         mixed = moved if mixed is None else jnp.where(part == sub, moved, mixed)
-                    out_ref[col, f, k, 16 * h + 8 * i:16 * h + 8 * i + 8, :] = mixed
-        store = pltpu.make_async_copy(
-            out_ref.at[col], out_hbm.at[0, :, :, :, pl.ds(128 * col, 128)], s_out.at[col])
-        store.start()
-        stores.append(store)
+                    out_ref[0, f, k, 16 * h + 8 * i:16 * h + 8 * i + 8, 128 * col:128 * col + 128] = mixed
 
     for flat in others():
         first_copy(flat).wait_send()
         second_copy(flat).wait_send()
-    for store in stores:
-        store.wait()
 
 
 def banded(az_count, density, velocity, pressure, offsets):
@@ -650,13 +654,12 @@
         functools.partial(kernel, az_count),
         out_shape=jax.ShapeDtypeStruct((1, 5) + density.shape[1:], f32),
         in_specs=[anywhere] * 4,
-        out_specs=anywhere,
+        out_specs=pl.BlockSpec(memory_space=pltpu.VMEM),
         scratch_shapes=[
             pltpu.SMEM(offsets.shape, jnp.int32),
             pltpu.VMEM(density.shape, f32),
             pltpu.VMEM(velocity.shape, f32),
             pltpu.VMEM(pressure.shape, f32),
-            pltpu.VMEM((4, 5, 2, 32, LANES), f32),
             pltpu.VMEM((chips, 5, 16, LANES), f32),
             pltpu.VMEM((chips, 5, 16, LANES), f32),
             pltpu.VMEM((chips, 5, 16, LANES), f32),
@@ -671,7 +674,7 @@
             pltpu.VMEM((3, 5, cells // 4, LANES), f32),
             pltpu.VMEM((5, 2 * cells + 8, LANES), f32),
             dma((chips,)), dma((chips,)), dma((chips,)), dma((chips,)),
-            dma((3, 2)), dma((3, 2)), dma((3,)), dma((3,)), dma((4,)), dma((4,)),
+            dma((3, 2)), dma((3, 2)), dma((3,)), dma((3,)), dma((4,)),
         ],
         compiler_params=pltpu.CompilerParams(
             collective_id=0, has_side_effects=True, vmem_limit_bytes=56 * 2**20

time: 56.3 us -> 57.5 us (1.021)
  the two profiles are of different devices: /device:TPU:14 before, /device:TPU:0 now
where the time goes in v3:
time: 57.5 us; the launch traced here: 57.4 us
  Pallas kernels  55.4 us (96%)
  local copies, waits for them, and re-layouts  1.97 us (3%)
    pallas_call x1, Pallas kernels, banded(): pl.pallas_call(functools.partial(kernel, az_count), out_shape=jax.ShapeDt...  55.4 us
    unnamed x1, local copies, waits for them, and re-layouts  1.97 us

profile of v3, /device:TPU:0, one launch (start us, length us, event | category | flops | bytes accessed | tf_op | source)
XLA Modules:
  0.0 57.4 jit_solution(11633652045451482708)
XLA Ops:
  0.0 55.4 %shard_map.46 = f32[1,5,2,32,512]{4,3,2,1,0:T(8,128)} custom-call(s32[3]{0:T(128)} %off_hbm.1, f32[1,2,32,512]{3,2,1,0:T(8,128)} %den_hbm.1, f32[1,3,2,32,512]{4,3,2,1,0:T(8,128)} %vel_hbm.1, f32[1,2,32,512]{3,2,1,0:T(8,128)} %pre_hbm.1), custom_call_target="tpu_custom_call" | custom-call | tf_op jit(solution)/shard_map/pallas_call | solution.py:653
  55.4 2.0 %copy.6 = f32[1,5,2,32,512]{4,3,2,1,0:T(8,128)} copy(f32[1,5,2,32,512]{4,3,2,1,0:T(8,128)} %shard_map.46) | data formatting | bytes 1310720

commit v4 on v3

--- a/solution.py
+++ b/solution.py
@@ -323,11 +323,7 @@
     radius = turn_cells / (2.0 * math.pi) + (band * 32 + inner).astype(jnp.float32) + 0.5
     inverse = 1.0 / radius
     c_turn = inverse * (0.5 / dtheta)
-    c_out = 0.5 * (radius + 1.0) * inverse
-    c_in = 0.5 * (radius - 1.0) * inverse
     l_turn = (inverse * (1.0 / dtheta)) * (inverse * (1.0 / dtheta))
-    l_out = (radius + 0.5) * inverse
-    l_in = (radius - 0.5) * inverse
     l_mid = 2.0 * l_turn + (2.0 + 2.0 * AXIAL_CURVE)
     inverse2 = inverse * inverse
     c_cross = inverse2 * (VISCOSITY / dtheta)
@@ -336,10 +332,10 @@
     edge_c = (0.5 * (r_low - 1.0) / r_low, -0.5 * (r_high + 1.0) / r_high)
     edge_l = ((r_low - 0.5) / r_low, (r_high + 0.5) / r_high)
     zero = jnp.zeros((TILE, LANES), jnp.float32)
-    c_in = jnp.where(inner == 0, zero, c_in)
-    l_in = jnp.where(inner == 0, zero, l_in)
-    c_out = jnp.where(inner == 31, zero, c_out)
-    l_out = jnp.where(inner == 31, zero, l_out)
+    give_next = jnp.where(inner == 31, zero, 0.5 * radius / (radius + 1.0))
+    give_last = jnp.where(inner == 0, zero, -0.5 * radius / (radius - 1.0))
+    drag_next = jnp.where(inner == 31, zero, (radius + 0.5) / (radius + 1.0))
+    drag_last = jnp.where(inner == 0, zero, (radius - 0.5) / (radius - 1.0))
 
     def pack(tiles_of, a, slot):
         group = a // quarter
@@ -402,38 +398,48 @@
         keep, fresh = RUNGE_KUTTA[step]
         for t in range(tiles):
             row0 = a * 32 + t * 8
-            mid, tl, th, rl, rr, zl, zh = [], [], [], [], [], [], []
-            for f in range(5):
-                c = prim[which, f, pl.ds(pl.multiple_of(row0 + 8, 8), 8), :]
-                mid.append(c)
-                tl.append(prim[which, f, pl.ds(row0 + 7, 8), :])
-                th.append(prim[which, f, pl.ds(row0 + 9, 8), :])
-                rl.append(pltpu.roll(c, 1, axis=1))
-                rr.append(pltpu.roll(c, 127, axis=1))
-                zl.append(jnp.where(part == 0, c, pltpu.roll(c, 32, axis=1)))
-                zh.append(jnp.where(part == 3, zero, pltpu.roll(c, 96, axis=1)))
+            mid = [prim[which, f, pl.ds(pl.multiple_of(row0 + 8, 8), 8), :] for f in range(5)]
+            rho, vt, vr, vz, temp = mid
+            heat = 3.5 * temp + 0.5 * (vt * vt + vr * vr + vz * vz)
+            press = rho * temp
+            spin = rho * vt
+            total = [
+                None,
+                -inverse * (spin * vr) - (VISCOSITY * (l_mid + inverse2)) * vt,
+                inverse * (spin * vt + press) - (VISCOSITY * (l_mid + inverse2)) * vr,
+                -(VISCOSITY * l_mid) * vz,
+                -(CONDUCTION * l_mid) * temp,
+            ]
+            m = rho * vz
+            terms = [m, m * vt, m * vr, m * vz + press, m * heat]
+            for f in range(5):
+                up, down = terms[f], -terms[f]
+                if f:
+                    worn = (AXIAL_CURVE * drag[f]) * mid[f]
+                    up, down = worn + terms[f], worn - terms[f]
+                value = (jnp.where(part == 0, up, pltpu.roll(up, 32, axis=1))
+                         + jnp.where(part == 3, zero, pltpu.roll(down, 96, axis=1)))
+                total[f] = value if total[f] is None else total[f] + value
+            m = rho * vr
+            terms = [m, m * vt, m * vr + press, m * vz, m * heat]
+            for f in range(5):
+                out, back = give_next * terms[f], give_last * terms[f]
+                if f:
+                    worn = drag[f] * mid[f]
+                    out, back = out + drag_next * worn, back + drag_last * worn
+                total[f] = total[f] + pltpu.roll(out, 1, axis=1) + pltpu.roll(back, 127, axis=1)
+            tl = [prim[which, f, pl.ds(row0 + 7, 8), :] for f in range(5)]
+            th = [prim[which, f, pl.ds(row0 + 9, 8), :] for f in range(5)]
             ftl, fth = flux(tl, 0), flux(th, 0)
-            frl, frh = flux(rl, 1), flux(rr, 1)
-            fzl, fzh = flux(zl, 2), flux(zh, 2)
-            total = [
-                c_turn * (ftl[f] - fth[f]) + (c_in * frl[f] - c_out * frh[f]) + (fzl[f] - fzh[f])
-                for f in range(5)
-            ]
-
-            def lap(n):
-                return (l_turn * (th[n] + tl[n]) + (l_out * rr[n] + l_in * rl[n])
-                        + AXIAL_CURVE * (zh[n] + zl[n]) - l_mid * mid[n])
-
-            rho, vt, vr, vz, temp = mid
-            total[1] = (total[1] - rho * vt * vr * inverse
-                        + VISCOSITY * (lap(1) - vt * inverse2) + c_cross * (th[2] - tl[2]))
-            total[2] = (total[2] + rho * (vt * vt + temp) * inverse
-                        + VISCOSITY * (lap(2) - vr * inverse2) - c_cross * (th[1] - tl[1]))
-            total[3] = total[3] + VISCOSITY * lap(3)
-            total[4] = total[4] + CONDUCTION * lap(4)
+            for f in range(5):
+                total[f] = total[f] + c_turn * (ftl[f] - fth[f])
+                if f:
+                    total[f] = total[f] + (drag[f] * l_turn) * (th[f] + tl[f])
+            total[1] = total[1] + c_cross * (th[2] - tl[2])
+            total[2] = total[2] - c_cross * (th[1] - tl[1])
             rows = pl.ds(pl.multiple_of(row0, 8), 8)
             for f in range(5):
-                value = fresh * (now[f, rows, :] + TIME_STEP * total[f])
+                value = fresh * now[f, rows, :] + (fresh * TIME_STEP) * total[f]
                 if keep:
                     value = value + keep * base[f, rows, :]
                 now[f, rows, :] = value
@@ -509,13 +515,13 @@
                 inside((az + spread(j + az_count - 2, half)) % az_count, 0)
                 return carry
 
-            lax.fori_loop(0, 2, rest, 0)
+            lax.fori_loop(0, 2, rest, 0, unroll=2)
         else:
             def sweep(a, carry, step=step):
                 inside((az + spread(a, half)) % az_count, step)
                 return carry
 
-            lax.fori_loop(0, az_count if step == 1 else half, sweep, 0)
+            lax.fori_loop(0, az_count if step == 1 else half, sweep, 0, unroll=2)
         for copy in copies:
             copy.wait()
         weight = TIME_STEP * RUNGE_KUTTA[step][1]
@@ -549,7 +555,7 @@
                     ghost[f, pl.ds(pl.multiple_of(turn_cells + place, 8), 8), :] = moved
             return carry
 
-        lax.fori_loop(0, 4 * quarter, slide, 0)
+        lax.fori_loop(0, 4 * quarter, slide, 0, unroll=4)
         shift = off_ref[step]
         shift = jnp.where(row == 0, shift, turn_cells - shift)
 
@@ -608,7 +614,7 @@
                     recv2[band] = send2[me]
             return carry
 
-        lax.fori_loop(0, az_count, edges, 0)
+        lax.fori_loop(0, az_count, edges, 0, unroll=1 if step == 2 else 2)
 
     for col in range(4):
         for sub in range(4):
@@ -649,7 +655,7 @@
     cells = 32 * az_count
     f32 = jnp.float32
     dma = pltpu.SemaphoreType.DMA
-    anywhere = pl.BlockSpec(memory_space=pl.ANY)
+    anywhere = pl.BlockSpec(memory_space=pltpu.HBM)
     return pl.pallas_call(
         functools.partial(kernel, az_count),
         out_shape=jax.ShapeDtypeStruct((1, 5) + density.shape[1:], f32),

time: 57.5 us -> 55.7 us (0.969)
  Pallas kernels: 55.4 us -> 53.6 us
    pallas_call x1, Pallas kernels: 55.4 us -> 53.6 us  [banded(): pl.pallas_call(functools.partial(kernel, az_count), out_shape=jax.ShapeDt...]
where the time goes in v4:
time: 55.7 us; the launch traced here: 55.6 us
  Pallas kernels  53.6 us (96%)
  local copies, waits for them, and re-layouts  1.97 us (4%)
    pallas_call x1, Pallas kernels, banded(): pl.pallas_call(functools.partial(kernel, az_count), out_shape=jax.ShapeDt...  53.6 us
    unnamed x1, local copies, waits for them, and re-layouts  1.97 us

profile of v4, /device:TPU:0, one launch (start us, length us, event | category | flops | bytes accessed | tf_op | source)
XLA Modules:
  0.0 55.6 jit_solution(1138622483570699290)
XLA Ops:
  0.0 53.6 %shard_map.46 = f32[1,5,2,32,512]{4,3,2,1,0:T(8,128)} custom-call(s32[3]{0:T(128)} %off_hbm.1, f32[1,2,32,512]{3,2,1,0:T(8,128)} %den_hbm.1, f32[1,3,2,32,512]{4,3,2,1,0:T(8,128)} %vel_hbm.1, f32[1,2,32,512]{3,2,1,0:T(8,128)} %pre_hbm.1), custom_call_target="tpu_custom_call" | custom-call | tf_op jit(solution)/shard_map/pallas_call | solution.py:659
  53.6 2.0 %copy.6 = f32[1,5,2,32,512]{4,3,2,1,0:T(8,128)} copy(f32[1,5,2,32,512]{4,3,2,1,0:T(8,128)} %shard_map.46) | data formatting | bytes 1310720

commit v5 on v4

--- a/solution.py
+++ b/solution.py
@@ -226,16 +226,12 @@
     return ax, deep * 2 + side
 
 
-def spread(j, half):
-    return half + (j % 2) * ((j + 1) // 2) - (1 - j % 2) * (j // 2)
-
-
 def kernel(
     az_count,
     off_hbm, den_hbm, vel_hbm, pre_hbm, out_ref,
     off_ref, den_ref, vel_ref, pre_ref,
-    send1, recv1, send2, recv2, base, now, prim, halo_out, halo_in, halo, plane_out, plane_in, ghost,
-    s1, r1, s2, r2, sh, rh, sp, rp, s_in,
+    send1, relay1, recv1, send2, relay2, recv2, base, now, prim, halo_out, halo_in, halo, plane_out, plane_in, ghost,
+    sz1, rz1, sf1, r1, sz2, rz2, sf2, r2, sh, rh, sp, rp, s_in,
 ):
     chips = 2 * az_count
     half = az_count // 2
@@ -245,11 +241,11 @@
     row = lax.axis_index("row")
     ax = lax.axis_index("ax")
     az = lax.axis_index("az")
-    me = ax * az_count + az
+    level, corner = az // 2, 2 * (az % 2) + ax
     band = band_of(ax, az, wide)
 
-    def chip_id(flat):
-        return (row, flat // az_count, flat % az_count)
+    def place(to_level, to_corner):
+        return (row, to_corner % 2, 2 * to_level + to_corner // 2)
 
     def band_id(which):
         return (row,) + chip_of(which, wide)
@@ -262,8 +258,10 @@
     for load in loads:
         load.start()
     barrier = pltpu.get_barrier_semaphore()
-    for i in range(1, chips):
-        pl.semaphore_signal(barrier, inc=1, device_id=chip_id((me + i) % chips), device_id_type=PEER)
+    for i in range(1, wide):
+        pl.semaphore_signal(barrier, inc=1, device_id=place((level + i) % wide, corner), device_id_type=PEER)
+    for i in range(1, 4):
+        pl.semaphore_signal(barrier, inc=1, device_id=place(level, (corner + i) % 4), device_id_type=PEER)
     pl.semaphore_signal(barrier, inc=1, device_id=(1 - row, ax, az), device_id_type=PEER)
 
     lane = lax.broadcasted_iota(jnp.int32, (TILE, LANES), 1)
@@ -294,30 +292,29 @@
                         turn = (32 * (q - sub)) % 128
                         moved = pltpu.roll(source[q], turn, axis=1) if turn else source[q]
                         mixed = moved if mixed is None else jnp.where(part == q, moved, mixed)
-                    send1[4 * col + sub, f, 8 * i:8 * i + 8, :] = mixed
-
-    pl.semaphore_wait(barrier, chips)
-
-    def first_copy(flat):
+                    to_ax, to_az = chip_of(4 * col + sub, wide)
+                    send1[2 * to_az + to_ax, f, 8 * i:8 * i + 8, :] = mixed
+
+    pl.semaphore_wait(barrier, wide + 3)
+
+    def remote(src, dst, send_sem, recv_sem, to_level, to_corner):
         return pltpu.make_async_remote_copy(
-            src_ref=send1.at[band_of(flat // az_count, flat % az_count, wide)],
-            dst_ref=recv1.at[me],
-            send_sem=s1.at[flat],
-            recv_sem=r1.at[me],
-            device_id=chip_id(flat),
-            device_id_type=PEER,
-        )
-
-    def others():
-        for j in range(az_count):
-            for x in range(2):
-                offset = spread(j, half) % az_count
-                if offset or x:
-                    yield ((ax + x) % 2) * az_count + (az + az_count - offset) % az_count
-
-    for flat in others():
-        first_copy(flat).start()
-    recv1[me] = send1[band]
+            src_ref=src, dst_ref=dst, send_sem=send_sem, recv_sem=recv_sem,
+            device_id=place(to_level, to_corner), device_id_type=PEER)
+
+    def along1(to):
+        return remote(send1.at[pl.ds(4 * to, 4)], relay1.at[level], sz1.at[to], rz1.at[level], to, corner)
+
+    def across1(source, of_level, to):
+        return remote(source, recv1.at[4 * of_level + corner], sf1.at[of_level, to],
+                      r1.at[4 * of_level + corner], level, to)
+
+    for k in range(1, wide):
+        along1((level + wide - k) % wide).start()
+    for i in range(1, 4):
+        to = (corner + i) % 4
+        across1(send1.at[4 * level + to], level, to).start()
+    recv1[4 * level + corner] = send1[4 * level + corner]
 
     dtheta = 2.0 * math.pi / turn_cells
     radius = turn_cells / (2.0 * math.pi) + (band * 32 + inner).astype(jnp.float32) + 0.5
@@ -450,8 +447,8 @@
             h, i = t // 2, t % 2
             w = []
             for f in range(5):
-                c0 = recv1[a, f, 8 * i:8 * i + 8, :]
-                c1 = recv1[az_count + a, f, 8 * i:8 * i + 8, :]
+                c0 = recv1[2 * a, f, 8 * i:8 * i + 8, :]
+                c1 = recv1[2 * a + 1, f, 8 * i:8 * i + 8, :]
                 if h == 0:
                     w.append(jnp.where(part < 2, c0, pltpu.roll(c1, 64, axis=1)))
                 else:
@@ -469,41 +466,46 @@
         wrap(0, a, tiles_of)
         pack(tiles_of, a, 0)
 
-    def arrive(j, carry):
-        a = (az + spread(j, half)) % az_count
-        for x in range(2):
-            flat = x * az_count + a
-
-            @pl.when(flat != me)
+    def arrive(k, carry):
+        @pl.when(k < wide)
+        def _():
+            of_level = (level + k) % wide
+            remote(send1.at[pl.ds(4 * of_level, 4)], relay1.at[of_level], sz1.at[of_level],
+                   rz1.at[of_level], of_level, corner).wait_recv()
+            for i in range(1, 4):
+                to = (corner + i) % 4
+                across1(relay1.at[of_level, to], of_level, to).start()
+            recv1[4 * of_level + corner] = relay1[of_level, corner]
+
+        for n in range(2):
+            j = 2 * (k - 1) + n
+            a = (2 * level + j) % az_count
+            for x in range(2):
+                of_corner = 2 * (a % 2) + x
+
+                @pl.when(of_corner != corner)
+                def _():
+                    slot = 2 * a + x
+                    remote(send1.at[slot], recv1.at[slot], sf1.at[a // 2, of_corner], r1.at[slot],
+                           level, of_corner).wait_recv()
+
+            unpack(a)
+
+            @pl.when(j >= 2)
             def _():
-                pltpu.make_async_remote_copy(
-                    src_ref=send1.at[flat],
-                    dst_ref=recv1.at[flat],
-                    send_sem=s1.at[flat],
-                    recv_sem=r1.at[flat],
-                    device_id=chip_id(flat),
-                    device_id_type=PEER,
-                ).wait_recv()
-
-        unpack(a)
-
-        @pl.when(j >= 2)
-        def _():
-            inside((az + spread(j - 2, half)) % az_count, 0)
+                inside((2 * level + j + az_count - 1) % az_count, 0)
 
         return carry
 
-    lax.fori_loop(0, az_count, arrive, 0)
-
-    def second_copy(flat):
-        return pltpu.make_async_remote_copy(
-            src_ref=send2.at[flat],
-            dst_ref=recv2.at[band],
-            send_sem=s2.at[flat],
-            recv_sem=r2.at[band],
-            device_id=chip_id(flat),
-            device_id_type=PEER,
-        )
+    lax.fori_loop(1, wide + 1, arrive, 0)
+
+    def along2(a):
+        return remote(send2.at[pl.ds(2 * a, 2)], relay2.at[level, pl.ds(2 * (a % 2), 2)], sz2.at[a],
+                      rz2.at[level, a % 2], a // 2, corner)
+
+    def across2(source, of_level, to):
+        of_band = band_of(ax, 2 * of_level + az % 2, wide)
+        return remote(source, recv2.at[of_band], sf2.at[of_level, to], r2.at[of_band], level, to)
 
     signs = (1.0, -1.0, -1.0, -1.0, 1.0)
     for step in range(3):
@@ -512,13 +514,13 @@
             copy.start()
         if step == 0:
             def rest(j, carry):
-                inside((az + spread(j + az_count - 2, half)) % az_count, 0)
+                inside((2 * level + az_count - 1 + j) % az_count, 0)
                 return carry
 
             lax.fori_loop(0, 2, rest, 0, unroll=2)
         else:
             def sweep(a, carry, step=step):
-                inside((az + spread(a, half)) % az_count, step)
+                inside((2 * level + 2 + a) % az_count, step)
                 return carry
 
             lax.fori_loop(0, az_count if step == 1 else half, sweep, 0, unroll=2)
@@ -561,7 +563,7 @@
 
         def edges(j, carry, step=step, shift=shift):
             which = step % 2
-            a = j if step < 2 else (az + spread(j, half)) % az_count
+            a = j if step < 2 else (2 * level + 2 + j) % az_count
             if step == 2:
                 @pl.when(j >= half)
                 def _():
@@ -599,39 +601,57 @@
             for f in range(5):
                 for i in range(2):
                     upper, lower = states[i][f], states[2 + i][f]
-                    send2[a, f, 8 * i:8 * i + 8, :] = jnp.where(part < 2, upper, pltpu.roll(lower, 64, axis=1))
-                    send2[az_count + a, f, 8 * i:8 * i + 8, :] = jnp.where(
+                    send2[2 * a, f, 8 * i:8 * i + 8, :] = jnp.where(part < 2, upper, pltpu.roll(lower, 64, axis=1))
+                    send2[2 * a + 1, f, 8 * i:8 * i + 8, :] = jnp.where(
                         part < 2, pltpu.roll(upper, 64, axis=1), lower)
+            @pl.when(a // 2 != level)
+            def _():
+                along2(a).start()
+
             for x in range(2):
-                flat = x * az_count + a
-
-                @pl.when(flat != me)
+                to = 2 * (a % 2) + x
+
+                @pl.when((a // 2 == level) & (to != corner))
                 def _():
-                    second_copy(flat).start()
-
-                @pl.when(flat == me)
+                    across2(send2.at[2 * a + x], level, to).start()
+
+                @pl.when((a // 2 == level) & (to == corner))
                 def _():
-                    recv2[band] = send2[me]
+                    recv2[band] = send2[2 * a + x]
             return carry
 
         lax.fori_loop(0, az_count, edges, 0, unroll=1 if step == 2 else 2)
+
+    def pass_on(k, carry):
+        of_level = (level + wide - k) % wide
+        for n in range(2):
+            remote(send2.at[pl.ds(0, 2)], relay2.at[of_level, pl.ds(2 * n, 2)], sz2.at[0],
+                   rz2.at[of_level, n], of_level, corner).wait_recv()
+            for x in range(2):
+                to = 2 * n + x
+
+                @pl.when(to != corner)
+                def _():
+                    across2(relay2.at[of_level, to], of_level, to).start()
+
+                @pl.when(to == corner)
+                def _():
+                    recv2[band_of(ax, 2 * of_level + az % 2, wide)] = relay2[of_level, to]
+
+        return carry
+
+    lax.fori_loop(1, wide, pass_on, 0)
 
     for col in range(4):
         for sub in range(4):
             from_band = 4 * col + sub
             from_ax, from_az = chip_of(from_band, wide)
-            flat = from_ax * az_count + from_az
-
-            @pl.when(flat != me)
+            of_corner = 2 * (from_az % 2) + from_ax
+
+            @pl.when(of_corner != corner)
             def _():
-                pltpu.make_async_remote_copy(
-                    src_ref=send2.at[flat],
-                    dst_ref=recv2.at[from_band],
-                    send_sem=s2.at[flat],
-                    recv_sem=r2.at[from_band],
-                    device_id=chip_id(flat),
-                    device_id_type=PEER,
-                ).wait_recv()
+                remote(send2.at[0], recv2.at[from_band], sf2.at[from_az // 2, of_corner],
+                       r2.at[from_band], level, of_corner).wait_recv()
 
         for f in range(5):
             for i in range(2):
@@ -645,9 +665,16 @@
                         mixed = moved if mixed is None else jnp.where(part == sub, moved, mixed)
                     out_ref[0, f, k, 16 * h + 8 * i:16 * h + 8 * i + 8, 128 * col:128 * col + 128] = mixed
 
-    for flat in others():
-        first_copy(flat).wait_send()
-        second_copy(flat).wait_send()
+    for k in range(1, wide):
+        to = (level + k) % wide
+        along1(to).wait_send()
+        for n in range(2):
+            along2(2 * to + n).wait_send()
+    for of_level in range(wide):
+        for i in range(1, 4):
+            to = (corner + i) % 4
+            across1(send1.at[0], of_level, to).wait_send()
+            across2(send2.at[0], of_level, to).wait_send()
 
 
 def banded(az_count, density, velocity, pressure, offsets):
@@ -667,8 +694,10 @@
             pltpu.VMEM(velocity.shape, f32),
             pltpu.VMEM(pressure.shape, f32),
             pltpu.VMEM((chips, 5, 16, LANES), f32),
+            pltpu.VMEM((az_count // 2, 4, 5, 16, LANES), f32),
             pltpu.VMEM((chips, 5, 16, LANES), f32),
             pltpu.VMEM((chips, 5, 16, LANES), f32),
+            pltpu.VMEM((az_count // 2, 4, 5, 16, LANES), f32),
             pltpu.VMEM((chips, 5, 16, LANES), f32),
             pltpu.VMEM((5, cells, LANES), f32),
             pltpu.VMEM((5, cells, LANES), f32),
@@ -679,7 +708,8 @@
             pltpu.VMEM((3, 5, cells // 4, LANES), f32),
             pltpu.VMEM((3, 5, cells // 4, LANES), f32),
             pltpu.VMEM((5, 2 * cells + 8, LANES), f32),
-            dma((chips,)), dma((chips,)), dma((chips,)), dma((chips,)),
+            dma((4,)), dma((4,)), dma((4, 4)), dma((chips,)),
+            dma((az_count,)), dma((4, 2)), dma((4, 4)), dma((chips,)),
             dma((3, 2)), dma((3, 2)), dma((3,)), dma((3,)), dma((4,)),
         ],
         compiler_params=pltpu.CompilerParams(

time: 55.7 us -> 60.2 us (1.081); the launches traced: 55.6 us -> 59.4 us
  Pallas kernels: 53.6 us -> 57.4 us
    pallas_call x1, Pallas kernels: 53.6 us -> 57.4 us  [banded(): pl.pallas_call(functools.partial(kernel, az_count), out_shape=jax.ShapeDt...]
where the time goes in v5:
time: 60.2 us; the launch traced here: 59.4 us
  Pallas kernels  57.4 us (95%)
  local copies, waits for them, and re-layouts  1.97 us (3%)
    pallas_call x1, Pallas kernels, banded(): pl.pallas_call(functools.partial(kernel, az_count), out_shape=jax.ShapeDt...  57.4 us
    unnamed x1, local copies, waits for them, and re-layouts  1.97 us

profile of v5, /device:TPU:0, one launch (start us, length us, event | category | flops | bytes accessed | tf_op | source)
XLA Modules:
  0.0 59.4 jit_solution(8727825650027647287)
XLA Ops:
  0.0 57.4 %shard_map.46 = f32[1,5,2,32,512]{4,3,2,1,0:T(8,128)} custom-call(s32[3]{0:T(128)} %off_hbm.1, f32[1,2,32,512]{3,2,1,0:T(8,128)} %den_hbm.1, f32[1,3,2,32,512]{4,3,2,1,0:T(8,128)} %vel_hbm.1, f32[1,2,32,512]{3,2,1,0:T(8,128)} %pre_hbm.1), custom_call_target="tpu_custom_call" | custom-call | tf_op jit(solution)/shard_map/pallas_call | solution.py:686
  57.4 2.0 %copy.6 = f32[1,5,2,32,512]{4,3,2,1,0:T(8,128)} copy(f32[1,5,2,32,512]{4,3,2,1,0:T(8,128)} %shard_map.46) | data formatting | bytes 1310720

commit v6 on v4

--- a/solution.py
+++ b/solution.py
@@ -209,7 +209,7 @@
 LANES = 128
 TILE = 8
 PEER = pl.DeviceIdType.MESH
-RUNGE_KUTTA = ((0.0, 1.0), (0.75, 0.25), (1.0 / 3.0, 2.0 / 3.0))
+RUNGE_KUTTA = ((0.0, 1.0), (0.75, 0.25), (1.0, 2.0))
 
 
 def band_of(ax, az, wide):
@@ -232,10 +232,10 @@
 
 def kernel(
     az_count,
-    off_hbm, den_hbm, vel_hbm, pre_hbm, out_ref,
-    off_ref, den_ref, vel_ref, pre_ref,
+    off_hbm, den_hbm, vel_hbm, pre_hbm, out_hbm,
+    off_ref, den_ref, vel_ref, pre_ref, out_ref,
     send1, recv1, send2, recv2, base, now, prim, halo_out, halo_in, halo, plane_out, plane_in, ghost,
-    s1, r1, s2, r2, sh, rh, sp, rp, s_in,
+    s1, r1, s2, r2, sh, rh, sp, rp, s_in, s_out,
 ):
     chips = 2 * az_count
     half = az_count // 2
@@ -616,6 +616,7 @@
 
         lax.fori_loop(0, az_count, edges, 0, unroll=1 if step == 2 else 2)
 
+    stores = []
     for col in range(4):
         for sub in range(4):
             from_band = 4 * col + sub
@@ -643,11 +644,18 @@
                         turn = (32 * (sub - q)) % 128
                         moved = pltpu.roll(source[sub], turn, axis=1) if turn else source[sub]
                         mixed = moved if mixed is None else jnp.where(part == sub, moved, mixed)
-                    out_ref[0, f, k, 16 * h + 8 * i:16 * h + 8 * i + 8, 128 * col:128 * col + 128] = mixed
+                    out_ref[col, f, k, 16 * h + 8 * i:16 * h + 8 * i + 8, :] = mixed
+
+        store = pltpu.make_async_copy(
+            out_ref.at[col], out_hbm.at[0, :, :, :, pl.ds(128 * col, 128)], s_out.at[col])
+        store.start()
+        stores.append(store)
 
     for flat in others():
         first_copy(flat).wait_send()
         second_copy(flat).wait_send()
+    for store in stores:
+        store.wait()
 
 
 def banded(az_count, density, velocity, pressure, offsets):
@@ -660,12 +668,13 @@
         functools.partial(kernel, az_count),
         out_shape=jax.ShapeDtypeStruct((1, 5) + density.shape[1:], f32),
         in_specs=[anywhere] * 4,
-        out_specs=pl.BlockSpec(memory_space=pltpu.VMEM),
+        out_specs=anywhere,
         scratch_shapes=[
             pltpu.SMEM(offsets.shape, jnp.int32),
             pltpu.VMEM(density.shape, f32),
             pltpu.VMEM(velocity.shape, f32),
             pltpu.VMEM(pressure.shape, f32),
+            pltpu.VMEM((4, 5, 2, 32, LANES), f32),
             pltpu.VMEM((chips, 5, 16, LANES), f32),
             pltpu.VMEM((chips, 5, 16, LANES), f32),
             pltpu.VMEM((chips, 5, 16, LANES), f32),
@@ -680,7 +689,7 @@
             pltpu.VMEM((3, 5, cells // 4, LANES), f32),
             pltpu.VMEM((5, 2 * cells + 8, LANES), f32),
             dma((chips,)), dma((chips,)), dma((chips,)), dma((chips,)),
-            dma((3, 2)), dma((3, 2)), dma((3,)), dma((3,)), dma((4,)),
+            dma((3, 2)), dma((3, 2)), dma((3,)), dma((3,)), dma((4,)), dma((4,)),
         ],
         compiler_params=pltpu.CompilerParams(
             collective_id=0, has_side_effects=True, vmem_limit_bytes=56 * 2**20
@@ -691,7 +700,7 @@
 def whole_step(density, velocity, pressure, offsets):
     ax_count, az_count = lax.axis_size("ax"), lax.axis_size("az")
     if ax_count == 2 and az_count == 8 and density.shape == (1, 2, 32, 512):
-        return banded(az_count, density, velocity, pressure, offsets)
+        return banded(az_count, density, velocity, pressure, offsets) * (1.0 / 3.0)
     return body(density, velocity, pressure, offsets)
 
 

time: 55.7 us -> 55.6 us (level)
  other arithmetic: 0 us -> 1.99 us
  local copies, waits for them, and re-layouts: 1.97 us -> 0 us
    mul x0 -> x1, other arithmetic: none -> 1.99 us  [whole_step(): return banded(az_count, density, velocity, pressure, offsets) * (1.0 / 3.0)]
    unnamed x1 -> x0, local copies, waits for them, and re-layouts: 1.97 us -> none
where the time goes in v6:
time: 55.6 us; the launch traced here: 55.4 us
  Pallas kernels  53.4 us (96%)
  other arithmetic  1.99 us (4%)
    pallas_call x1, Pallas kernels, banded(): pl.pallas_call(functools.partial(kernel, az_count), out_shape=jax.ShapeDt...  53.4 us
    mul x1, other arithmetic, whole_step(): return banded(az_count, density, velocity, pressure, offsets) * (1.0 / 3.0)  1.99 us

profile of v6, /device:TPU:0, one launch (start us, length us, event | category | flops | bytes accessed | tf_op | source)
XLA Modules:
  0.0 55.4 jit_solution(9307603173169618154)
XLA Ops:
  0.0 53.4 %shard_map.46 = f32[1,5,2,32,512]{4,3,2,1,0:T(8,128)} custom-call(s32[3]{0:T(128)} %off_hbm.1, f32[1,2,32,512]{3,2,1,0:T(8,128)} %den_hbm.1, f32[1,3,2,32,512]{4,3,2,1,0:T(8,128)} %vel_hbm.1, f32[1,2,32,512]{3,2,1,0:T(8,128)} %pre_hbm.1), custom_call_target="tpu_custom_call" | custom-call | tf_op jit(solution)/shard_map/pallas_call | solution.py:667
  53.4 2.0 %broadcast_multiply_fusion = f32[1,5,2,32,512]{4,3,2,1,0:T(8,128)} fusion(f32[1,5,2,32,512]{4,3,2,1,0:T(8,128)} %shard_map.46), kind=kLoop, calls=%fused_computation | loop fusion | flops 163840 | bytes 1310720 | tf_op jit(solution)/shard_map/mul | solution.py:703

commit v7 on v6

--- a/solution.py
+++ b/solution.py
@@ -470,7 +470,7 @@
         pack(tiles_of, a, 0)
 
     def arrive(j, carry):
-        a = (az + spread(j, half)) % az_count
+        a = (az + spread(j, az_count)) % az_count
         for x in range(2):
             flat = x * az_count + a
 
@@ -489,7 +489,7 @@
 
         @pl.when(j >= 2)
         def _():
-            inside((az + spread(j - 2, half)) % az_count, 0)
+            inside((az + spread(j - 2, az_count)) % az_count, 0)
 
         return carry
 
@@ -512,7 +512,7 @@
             copy.start()
         if step == 0:
             def rest(j, carry):
-                inside((az + spread(j + az_count - 2, half)) % az_count, 0)
+                inside((az + spread(j + az_count - 2, az_count)) % az_count, 0)
                 return carry
 
             lax.fori_loop(0, 2, rest, 0, unroll=2)
@@ -521,7 +521,7 @@
                 inside((az + spread(a, half)) % az_count, step)
                 return carry
 
-            lax.fori_loop(0, az_count if step == 1 else half, sweep, 0, unroll=2)
+            lax.fori_loop(0, az_count if step == 1 else az_count - 2, sweep, 0, unroll=2)
         for copy in copies:
             copy.wait()
         weight = TIME_STEP * RUNGE_KUTTA[step][1]
@@ -563,7 +563,7 @@
             which = step % 2
             a = j if step < 2 else (az + spread(j, half)) % az_count
             if step == 2:
-                @pl.when(j >= half)
+                @pl.when(j >= az_count - 2)
                 def _():
                     inside(a, step)
 

time: 55.6 us -> 55.5 us (level)
  no operation moved by 1% of the time
where the time goes in v7:
time: 55.5 us; the launch traced here: 55.3 us
  Pallas kernels  53.3 us (96%)
  other arithmetic  1.99 us (4%)
    pallas_call x1, Pallas kernels, banded(): pl.pallas_call(functools.partial(kernel, az_count), out_shape=jax.ShapeDt...  53.3 us
    mul x1, other arithmetic, whole_step(): return banded(az_count, density, velocity, pressure, offsets) * (1.0 / 3.0)  1.99 us

profile of v7, /device:TPU:0, one launch (start us, length us, event | category | flops | bytes accessed | tf_op | source)
XLA Modules:
  0.0 55.3 jit_solution(691757320319333371)
XLA Ops:
  0.0 53.3 %shard_map.46 = f32[1,5,2,32,512]{4,3,2,1,0:T(8,128)} custom-call(s32[3]{0:T(128)} %off_hbm.1, f32[1,2,32,512]{3,2,1,0:T(8,128)} %den_hbm.1, f32[1,3,2,32,512]{4,3,2,1,0:T(8,128)} %vel_hbm.1, f32[1,2,32,512]{3,2,1,0:T(8,128)} %pre_hbm.1), custom_call_target="tpu_custom_call" | custom-call | tf_op jit(solution)/shard_map/pallas_call | solution.py:667
  53.3 2.0 %broadcast_multiply_fusion = f32[1,5,2,32,512]{4,3,2,1,0:T(8,128)} fusion(f32[1,5,2,32,512]{4,3,2,1,0:T(8,128)} %shard_map.46), kind=kLoop, calls=%fused_computation | loop fusion | flops 163840 | bytes 1310720 | tf_op jit(solution)/shard_map/mul | solution.py:703
